TPU v7x, 128 devices: a whole 4x4x4 slice. The times are simulated.
128 devices in a mesh: lev: 4 (over x), band: 32 (over z, y, core).
Axes of the slice: x: 4, y: 4, z: 4, core: 2. Of those that a mesh axis runs over, the one named last changes fastest.
Arguments:
- spectra: bfloat16 [4, 4, 2, 2, 2048, 2048], P('lev', None, None, None, 'band'), may hold values from -1 to 1
- legendre: bfloat16 [2048, 64, 2048], P('band'), may hold values from -0.0034179688 to 0.0034179688
- wave_order: int32 [2048], replicated, may hold values from 0 to 2047, each once
- cand_block: int32 [6144], P('band'), may hold values from 0 to 255
- cand_owner: int32 [6144, 1], P('band'), may hold values from 0 to 31; in each aligned block of 192 rows (0 to 191, 192 to 383, ...) at most 12 rows name the same one
Outputs:
- vorticity: float32 [4, 4, 128, 8192], P('lev', None, 'band')
- okubo_weiss: float32 [4, 4, 128, 8192], P('lev', None, 'band')
- track_fits: float32 [12288, 20], P('band')
Inputs may be any that keep to these rules, and one draw needn't show every extreme that they name: Each wavenumber appears once; slot s of spectra and legendre belongs to wavenumber wave_order[s]. `cand_owner`: among the 192 candidates of one band no owner is named more than 12 times, a bound that some block reaches.
All inputs are finite; a program needn't handle non-finite values.
Results may differ from a plain program's by a relative error of at most 0.0053.
Values may be sent and summed in bfloat16 or wider, within the bound.
A program may use at most 128 MiB of HBM per device.

v0:
```python
import math

import jax
import jax.numpy as jnp
from jax import lax
from jax.sharding import PartitionSpec as P

NLON = 8192
BLON = 128


def padded(block, sides, width):
    for axis, dim in sides:
        count = lax.axis_size(axis)
        forward = [(i, i + 1) for i in range(count - 1)]
        backward = [(target, source) for source, target in forward]
        low = lax.ppermute(
            lax.slice_in_dim(block, block.shape[dim] - width, None, axis=dim), axis, forward
        )
        high = lax.ppermute(lax.slice_in_dim(block, 0, width, axis=dim), axis, backward)
        block = jnp.concatenate([low, block, high], axis=dim)
    return block


def ortho_values(count):
    offset = jnp.arange(count, dtype=jnp.float32) - (count - 1) / 2.0
    constant = jnp.ones_like(offset)
    square = offset * offset - (count * count - 1) / 12.0
    cubic = offset * offset * offset - (3 * count * count - 7) / 20.0 * offset
    stacked = jnp.stack([constant, offset, square, cubic], 0)
    return stacked / jnp.sqrt(jnp.sum(stacked * stacked, axis=1, keepdims=True))


def fit_basis(row_count, col_count):
    across = ortho_values(col_count)
    upward = ortho_values(row_count)
    orders = ((0, 0), (1, 0), (0, 1), (2, 0), (1, 1), (0, 2), (3, 0), (2, 1), (1, 2), (0, 3))
    columns = [
        (upward[y_order][:, None] * across[x_order][None, :]).reshape(-1)
        for x_order, y_order in orders
    ]
    return jnp.stack(columns, 1)


def metric_fields(psi_field, chi_field, lat_index, lat_total, wave_total, lon_total):
    step_y = math.pi / (2.0 * wave_total)
    latitude = (lat_total / 2.0 - lat_index - 0.5) * step_y
    step_x = (jnp.cos(latitude) * (2.0 * math.pi / lon_total)).reshape(-1, 1)

    def second_parts(values):
        centre = values[..., 1:-1, :]
        upper_row = values[..., :-2, :]
        lower_row = values[..., 2:, :]
        along_x = (jnp.roll(centre, -1, -1) - 2.0 * centre + jnp.roll(centre, 1, -1)) / (
            step_x * step_x
        )
        along_y = (upper_row - 2.0 * centre + lower_row) / (step_y * step_y)
        mixed_xy = (
            jnp.roll(upper_row, -1, -1)
            - jnp.roll(upper_row, 1, -1)
            - jnp.roll(lower_row, -1, -1)
            + jnp.roll(lower_row, 1, -1)
        ) / (4.0 * step_x * step_y)
        return (along_x, along_y, mixed_xy)

    psi_xx, psi_yy, psi_xy = second_parts(psi_field)
    chi_xx, chi_yy, chi_xy = second_parts(chi_field)
    vorticity = psi_xx + psi_yy
    strain_normal = -2.0 * psi_xy + chi_xx - chi_yy
    strain_shear = psi_xx - psi_yy + 2.0 * chi_xy
    okubo_weiss = (
        strain_normal * strain_normal + strain_shear * strain_shear - vorticity * vorticity
    )
    return (vorticity, okubo_weiss)


def longitude_synthesis(coeffs, wave_order, lon_total):
    row_total, slot_total, time_count, field_count, parts_count = coeffs.shape
    inner_width = 128
    outer_count = lon_total // inner_width
    high_count = slot_total // outer_count
    highest = lax.Precision.HIGHEST
    slot_of_wave = (
        jnp.zeros((slot_total,), jnp.int32)
        .at[wave_order]
        .set(jnp.arange(slot_total, dtype=jnp.int32))
    )
    ordered = jnp.take(coeffs, slot_of_wave, axis=1).astype(jnp.float32)
    waves = jnp.arange(slot_total, dtype=jnp.int32)
    weight = jnp.where(waves == 0, 1.0, 2.0).astype(jnp.float32)
    ordered = (ordered * weight[None, :, None, None, None]).reshape(
        row_total, high_count, outer_count, time_count, field_count, parts_count
    )
    real_in = ordered[..., 0]
    imag_in = ordered[..., 1]
    cells = jnp.arange(inner_width, dtype=jnp.int32)
    first_index = waves[:, None] * cells[None, :] % lon_total
    first_angle = (first_index.astype(jnp.float32) * (2.0 * math.pi / lon_total)).reshape(
        high_count, outer_count, inner_width
    )
    cos_first = jnp.cos(first_angle)
    sin_first = jnp.sin(first_angle)
    form = "rhltf,hlx->tfrlx"
    part_real = jnp.einsum(form, real_in, cos_first, precision=highest) - jnp.einsum(
        form, imag_in, sin_first, precision=highest
    )
    part_imag = jnp.einsum(form, real_in, sin_first, precision=highest) + jnp.einsum(
        form, imag_in, cos_first, precision=highest
    )
    lows = jnp.arange(outer_count, dtype=jnp.int32)
    second_index = lows[:, None] * lows[None, :] % outer_count
    second_angle = second_index.astype(jnp.float32) * (2.0 * math.pi / outer_count)
    cos_second = jnp.cos(second_angle)
    sin_second = jnp.sin(second_angle)
    second_form = "tfrlx,ly->tfryx"
    field = jnp.einsum(second_form, part_real, cos_second, precision=highest) - jnp.einsum(
        second_form, part_imag, sin_second, precision=highest
    )
    return field.reshape(time_count, field_count, row_total, lon_total)


def cut_blocks(fields_in, span_width):
    time_count, field_count, row_count, lon_count = fields_in.shape
    per_row = lon_count // span_width
    shaped = fields_in.reshape(time_count, field_count, row_count, per_row, span_width)
    return shaped.transpose(0, 3, 1, 2, 4).reshape(
        time_count * per_row, field_count, row_count * span_width
    )


def local(spectra, legendre, wave_order, cand_block, cand_owner):
    band_count = lax.axis_size("band")
    band_index = lax.axis_index("band")
    level_count = lax.axis_size("lev") * spectra.shape[0]
    slot_count, half_lat, degree_count = legendre.shape
    lat_total = 2 * half_lat
    row_count = lat_total // band_count
    time_count = spectra.shape[1]
    own_waves = lax.dynamic_slice_in_dim(wave_order, band_index * slot_count, slot_count)
    degree = jnp.arange(degree_count, dtype=jnp.int32)
    degree_f = degree.astype(jnp.float32)
    inverse = jnp.where(degree >= 1, -1.0 / jnp.maximum(degree_f * (degree_f + 1.0), 1.0), 0.0)
    kept_mask = degree[None, :] >= own_waves[:, None]
    parity = jnp.where((degree[None, :] - own_waves[:, None]) % 2 == 0, 1.0, -1.0).astype(
        jnp.float32
    )
    scaled = spectra[0].astype(jnp.float32) * jnp.where(kept_mask, inverse[None, :], 0.0)
    even_input = scaled.astype(jnp.bfloat16)
    odd_input = (scaled * parity).astype(jnp.bfloat16)
    paired = jnp.stack([even_input, odd_input], 0)
    summed = jnp.einsum(
        "gtfcsn,shn->ghstfc", paired, legendre, preferred_element_type=jnp.float32
    ).astype(jnp.bfloat16)
    fourier = jnp.concatenate([summed[0], jnp.flip(summed[1], 0)], 0).reshape(lat_total, -1)
    received = lax.all_to_all(fourier, "band", split_axis=0, concat_axis=1, tiled=True)
    centre_grid = longitude_synthesis(
        received.reshape(row_count, degree_count, time_count, 2, 2), wave_order, NLON
    )
    grid_field = padded(centre_grid, (("band", 2),), 1)
    lat_index = (band_index * row_count + jnp.arange(row_count, dtype=jnp.int32)).astype(
        jnp.float32
    )
    vorticity, okubo_weiss = metric_fields(
        grid_field[:, 0], grid_field[:, 1], lat_index, lat_total, degree_count, NLON
    )
    cand_count = cand_block.shape[0]
    capacity = 2 * cand_count // band_count
    owner_index = cand_owner[:, 0]
    onehot = (owner_index[:, None] == jnp.arange(band_count, dtype=jnp.int32)[None, :]).astype(
        jnp.int32
    )
    earlier = jnp.cumsum(onehot, 0) - onehot
    slot_index = jnp.sum(earlier * onehot, 1)
    position = owner_index * capacity + slot_index
    fit_table = fit_basis(row_count, BLON)
    total_vort, total_okubo = (
        lax.psum(vorticity.astype(jnp.bfloat16), "lev").astype(jnp.float32),
        lax.psum(okubo_weiss.astype(jnp.bfloat16), "lev").astype(jnp.float32),
    )
    mean_blocks = cut_blocks(jnp.stack([total_vort, total_okubo], 1) / level_count, BLON)
    picked = jnp.take(mean_blocks, cand_block, axis=0)
    outgoing = (
        jnp.zeros((band_count * capacity, 2, picked.shape[-1]), jnp.float32)
        .at[position]
        .set(picked)
    )
    arrived = lax.all_to_all(
        outgoing.astype(jnp.bfloat16), "band", split_axis=0, concat_axis=0, tiled=True
    ).astype(outgoing.dtype)
    track_fits = jnp.einsum(
        "qfp,pb->qfb", arrived, fit_table, precision=lax.Precision.HIGHEST
    ).reshape(-1, 20)
    return (vorticity[None], okubo_weiss[None], track_fits)


def solution(mesh):
    placed = (
        P("lev", None, None, None, "band", None),
        P("band", None, None),
        P(),
        P("band"),
        P("band", None),
    )
    return jax.shard_map(
        local,
        mesh=mesh,
        in_specs=placed,
        out_specs=(P("lev", None, "band", None), P("lev", None, "band", None), P("band", None)),
        check_vma=False,
    )
```

profile of v0, /device:TPU:1, one launch (start us, length us, event | category | flops | bytes accessed | tf_op | source)
XLA Modules:
  0.0 293.1 jit_solution(259065998685821535)
XLA Ops:
  7.2 0.8 dynamic_slice.3
  8.0 0.3 fusion.61
  8.3 8.8 %fusion.5 = (bf16[1,4,2,2,64,2048]{5,1,3,2,0,4:T(4,128)(2,1)}, bf16[1,4,2,2,64,2048]{5,1,3,2,0,4:T(4,128)(2,1)}) fusion(f32[64,2048]{1,0:T(8,128)S(1)} %get-tuple-element.62, bf16[1,4,2,2,64,2048]{5,4,3,2,1,0:T(8,128)(2,1)} %param.5, f32[64,2048]{1,0:T(8,128)S(1)} %get-tuple-element.63), kind=kLoop, calls=%fused_computation.11 | loop fusion | flops 10485760 | bytes 13631488 | tf_op jit(solution)/shard_map/convert_element_type | solution.py:148
  17.1 13.0 %fusion.14 = bf16[2,64,64,4,2,2]{1,3,5,4,0,2:T(4,128)(2,1)S(1)} fusion(bf16[64,64,2048]{2,1,0:T(8,128)(2,1)} %param.6, bf16[1,4,2,2,64,2048]{5,1,3,2,0,4:T(4,128)(2,1)} %get-tuple-element.11, bf16[1,4,2,2,64,2048]{5,1,3,2,0,4:T(4,128)(2,1)} %get-tuple-element.10), kind=kOutput, calls=%fused_computation.23 | convolution fusion | flops 553779200 | bytes 25427968 | tf_op jit(solution)/shard_map/gtfcsn,shn->ghstfc/dot_general | solution.py:151
  30.1 0.2 fusion.117
  30.3 0.7 rev.4
  31.0 0.2 copy.53
  31.2 0.2 copy.52
  31.4 0.1 pad_maximum_fusion.1
  31.6 0.1 copy.54
  31.7 0.8 all_to_all.15
  32.5 9.6 %all-to-all-start = ((bf16[32,4,1024]{2,1,0:T(4,128)(2,1)}), bf16[32,4,1024]{2,1,0:T(4,128)(2,1)S(1)}, u32[]{:S(2)}, u32[]{:S(2)}) async-start(bf16[32,4,1024]{2,1,0:T(4,128)(2,1)} %all_to_all.15), calls=%async_computation | async-start | bytes 524288 | tf_op jit(solution)/shard_map/all_to_all | solution.py:155
  42.2 8.2 %scatter_custom_fusion = s32[2048]{0:T(1024)S(1)} fusion(s32[2048]{0:T(1024)S(1)} %compare_select_fusion.1, s32[2048]{0:T(1024)S(1)} %iota.99, s32[]{:T(128)} %constant.66.clone.1), kind=kCustom, calls=%fused_computation.128 | custom fusion | bytes 8196 | tf_op jit(solution)/shard_map/scatter | solution.py:86
  50.6 0.6 reduce-window.6
  51.2 0.2 slice_reduce_fusion
  51.4 0.1 bitcast_bitcast_fusion
  51.6 0.2 multiply_reduce_fusion.1
  51.8 0.1 broadcast_divide_fusion.1
  51.8 0.2 multiply_reduce_fusion
  52.0 0.1 broadcast_divide_fusion
  52.1 0.1 broadcast_in_dim.89
  52.2 0.1 copy.50
  52.3 0.1 broadcast_multiply_fusion
  52.4 5.7 %copy.55 = bf16[4,32,1024]{0,2,1:T(8,128)(2,1)} copy(bf16[4,32,1024]{2,0,1:T(4,128)(2,1)S(1)} %bitcast.125) | data formatting | bytes 524288 | tf_op jit(solution)/shard_map/all_to_all | solution.py:155
  58.0 53.4 %copy.56 = bf16[4,2048,4,2,2]{2,0,4,3,1:T(4,128)(2,1)} copy(bf16[4,2048,4,2,2]{0,4,3,2,1:T(2,128)(2,1)} %bitcast.124) | data formatting | bytes 524288 | tf_op jit(solution)/shard_map/reshape | solution.py:157
  111.5 24.4 %gather_fusion = bf16[2048,4,4,2,2]{2,1,4,3,0:T(4,128)(2,1)} fusion(bf16[4,2048,4,2,2]{2,0,4,3,1:T(4,128)(2,1)} %copy.56, s32[2048]{0:T(1024)S(1)} %fusion.80), kind=kCustom, calls=%fused_computation | custom fusion | bytes 532480 | tf_op jit(solution)/shard_map/jit(_take)/gather | solution.py:88
  135.9 12.4 %copy.57 = bf16[4,32,64,4,2,2]{2,1,5,4,3,0:T(8,128)(2,1)S(1)} copy(bf16[4,32,64,4,2,2]{3,0,5,4,2,1:T(4,128)(2,1)} %bitcast.123) | data formatting | bytes 524288 | tf_op jit(solution)/shard_map/jit(_take)/gather | solution.py:88
  148.3 0.2 convert_multiply_fusion.1
  148.5 0.1 slice_bitcast_fusion.2
  148.6 1.1 copy.58
  149.7 7.1 %fusion.25 = f32[64,128,4,4,2]{1,3,4,2,0:T(4,128)} fusion(f32[4,32,64,4,2]{1,3,4,0,2:T(4,128)S(1)} %copy.58, s32[32,64]{0,1:T(8,128)S(1)} %copy.50), kind=kOutput, calls=%fused_computation.32 | convolution fusion | flops 104333312 | bytes 1318912 | tf_op jit(solution)/shard_map/rhltf,hlx->tfrlx/dot_general | solution.py:107
  156.8 7.1 %fusion.23 = f32[64,128,4,4,2]{1,3,4,2,0:T(4,128)} fusion(f32[4,32,64,4,2]{1,3,4,0,2:T(4,128)S(1)} %copy.58, s32[32,64]{0,1:T(8,128)S(1)} %copy.50), kind=kOutput, calls=%fused_computation.30 | convolution fusion | flops 104333312 | bytes 1318912 | tf_op jit(solution)/shard_map/rhltf,hlx->tfrlx/dot_general | solution.py:104
  163.9 1.1 copy.59
  165.1 7.4 %fusion.7 = f32[4,2,4,64,128]{4,0,1,2,3:T(4,128)S(1)} fusion(f32[64,128,4,4,2]{1,3,4,2,0:T(4,128)} %fusion.25, f32[4,32,64,4,2]{1,3,4,0,2:T(4,128)S(1)} %copy.59, s32[32,64]{0,1:T(8,128)S(1)} %copy.50), kind=kOutput, calls=%fused_computation.19 | convolution fusion | flops 104595456 | bytes 2367488 | tf_op jit(solution)/shard_map/rhltf,hlx->tfrlx/dot_general | solution.py:107
  172.4 7.6 %fusion.8 = f32[4,2,4,64,128]{4,0,1,2,3:T(4,128)S(1)} fusion(f32[64,128,4,4,2]{1,3,4,2,0:T(4,128)} %fusion.23, f32[4,32,64,4,2]{1,3,4,0,2:T(4,128)S(1)} %copy.59, s32[32,64]{0,1:T(8,128)S(1)} %copy.50), kind=kOutput, calls=%fused_computation.21 | convolution fusion | flops 104595456 | bytes 2367488 | tf_op jit(solution)/shard_map/rhltf,hlx->tfrlx/dot_general | solution.py:104
  180.1 1.7 fusion.29
  181.7 1.7 fusion.6
  183.4 0.4 reshape.451
  183.8 0.5 fusion.116
  184.3 3.5 %collective-permute-start = (f32[4,2,1,8192]{3,2,0,1:T(1,128)S(1)}, f32[4,2,1,8192]{3,2,0,1:T(1,128)S(1)}, u32[]{:S(2)}, u32[]{:S(2)}) collective-permute-start(f32[4,2,1,8192]{3,2,0,1:T(1,128)S(1)} %get-tuple-element.38), channel_id=1, source_target_pairs={{0,1},{1,2},{2,3},{3,4},{4,5},{5,6},{6,7},{7,8},{8,9},{9,10},{10,1... | collective-permute-start | bytes 786440 | tf_op jit(solution)/shard_map/ppermute | solution.py:17
  187.8 1.9 collective-permute-start.1
  189.8 0.1 stack.38
  189.9 1.2 collective-permute-done
  191.1 4.4 %collective-permute-done.1 = f32[4,2,1,8192]{3,2,0,1:T(1,128)S(1)} collective-permute-done((f32[4,2,1,8192]{3,2,0,1:T(1,128)S(1)}, f32[4,2,1,8192]{3,2,0,1:T(1,128)S(1)}, u32[]{:S(2)}, u32[]{:S(2)}) %collective-permute-start.1) | collective-permute-done | bytes 262176 | tf_op jit(solution)/shard_map/ppermute | solution.py:20
  195.5 0.7 pad_maximum_fusion
  196.2 0.1 slice_bitcast_fusion
  196.4 0.1 fusion.113
  196.5 2.3 fusion.112
  198.8 1.3 convert_bitcast_fusion.1
  200.1 2.9 %convert_bitcast_fusion = (bf16[4,1,4,64,128]{4,2,3,0,1:T(4,128)(2,1)}, f32[4,4,8192]{2,1,0:T(4,128)}) fusion(f32[4,4,8192]{2,1,0:T(4,128)S(1)} %get-tuple-element.7, f32[4,4,8192]{2,1,0:T(4,128)S(1)} %get-tuple-element.6, f32[4,4,8191]{2,1,0:T(4,128)S(1)} %get-tuple-element.65, f32[4,4,1]{2,1,0:T(4,128)S(1)} %get-tuple-element.70, ...), kind=kLoop, calls=%fused_computation.88 | loop fusion | flops 4980736 | bytes 8650784 | tf_op jit(solution)/shard_map/stack | solution.py:180
  203.1 43.4 %all-reduce.4.cloned.1.call-done = (bf16[4,1,4,64,128]{4,2,3,0,1:T(4,128)(2,1)}, bf16[4,1,4,64,128]{4,2,3,0,1:T(4,128)(2,1)}) async-done(((bf16[4,1,4,64,128]{4,2,3,0,1:T(4,128)(2,1)}, bf16[4,1,4,64,128]{4,2,3,0,1:T(4,128)(2,1)}), (bf16[4,1,4,64,128]{4,2,3,0,1:T(4,128)(2,1)}, bf16[4,1,4,64,128]{4,2,3,0,1:T(4,128)(2,1)})) %all-reduce.4.cloned.1.call-update) | async-done | bytes 524304 | tf_op jit(solution)/shard_map/psum | solution.py:178
  246.6 1.3 multiply_bitcast_fusion
  247.9 0.4 reshape.454
  248.3 0.8 copy.71
  249.1 2.4 gather_fusion.1
  251.5 1.6 broadcast_select_fusion
  253.1 0.4 broadcast_in_dim.101
  253.5 6.2 %scatter_fusion = f32[384,2,512]{2,1,0:T(2,128)S(1)} fusion(f32[384,2,512]{2,1,0:T(2,128)S(1)} %broadcast_in_dim.101, s32[192]{0:T(256)S(1)} %bitcast.141, f32[192,2,512]{2,1,0:T(2,128)S(1)} %broadcast_select_fusion), kind=kCustom, calls=%fused_computation.3 | custom fusion | bytes 2360064 | tf_op jit(solution)/shard_map/scatter | solution.py:185
  259.7 1.4 convert_element_type.86
  261.1 9.5 %all-to-all-start.1 = ((bf16[384,2,512]{2,1,0:T(2,128)(2,1)}), bf16[384,2,512]{2,1,0:T(2,128)(2,1)S(1)}, u32[]{:S(2)}, u32[]{:S(2)}) async-start(bf16[384,2,512]{2,1,0:T(2,128)(2,1)} %convert_element_type.86), calls=%async_computation.1 | async-start | bytes 1572864 | tf_op jit(solution)/shard_map/all_to_all | solution.py:187
  270.6 0.9 add_bitcast_fusion.1
  271.6 13.3 %all-to-all-done.1 = bf16[384,2,512]{2,1,0:T(2,128)(2,1)S(1)} async-done(((bf16[384,2,512]{2,1,0:T(2,128)(2,1)}), bf16[384,2,512]{2,1,0:T(2,128)(2,1)S(1)}, u32[]{:S(2)}, u32[]{:S(2)}) %all-to-all-start.1) | async-done | bytes 786464 | tf_op jit(solution)/shard_map/all_to_all | solution.py:187
  284.9 0.7 fusion.34
  285.6 0.6 reshape.455
  (35 shorter events, 0.4 us)
Async XLA Ops:
  17.1 25.1 %copy-start.1 = (s32[2048]{0:T(1024)S(1)}, s32[2048]{0:T(1024)}, u32[]{:S(2)}) copy-start(s32[2048]{0:T(1024)} %param.7) | copy-start | bytes 24580
  17.1 33.5 %copy-start = (s32[192,1]{0,1:T(1,128)S(1)}, s32[192,1]{0,1:T(1,128)}, u32[]{:S(2)}) copy-start(s32[192,1]{0,1:T(1,128)} %param.9) | copy-start | bytes 2308
  32.5 19.8 %all-to-all-start = ((bf16[32,4,1024]{2,1,0:T(4,128)(2,1)}), bf16[32,4,1024]{2,1,0:T(4,128)(2,1)S(1)}, u32[]{:S(2)}, u32[]{:S(2)}) async-start(bf16[32,4,1024]{2,1,0:T(4,128)(2,1)} %all_to_all.15), calls=%async_computation | async-start | bytes 524288 | tf_op jit(solution)/shard_map/all_to_all | solution.py:155
  42.2 204.4 %all-reduce.4.cloned.1.call-start = ((), (), s32[]{:S(2)}) async-start(), calls=%async_computation.2 | async-start | bytes 1048576 | tf_op jit(solution)/shard_map/psum | solution.py:178
  165.1 24.8 %copy-start.2 = (s32[192]{0:T(256)S(1)}, s32[192]{0:T(256)}, u32[]{:S(2)}) copy-start(s32[192]{0:T(256)} %param.8) | copy-start | bytes 2308
  184.3 6.8 %collective-permute-start = (f32[4,2,1,8192]{3,2,0,1:T(1,128)S(1)}, f32[4,2,1,8192]{3,2,0,1:T(1,128)S(1)}, u32[]{:S(2)}, u32[]{:S(2)}) collective-permute-start(f32[4,2,1,8192]{3,2,0,1:T(1,128)S(1)} %get-tuple-element.38), channel_id=1, source_target_pairs={{0,1},{1,2},{2,3},{3,4},{4,5},{5,6},{6,7},{7,8},{8,9},{9,10},{10,1... | collective-permute-start | bytes 786440 | tf_op jit(solution)/shard_map/ppermute | solution.py:17
  187.8 7.7 %collective-permute-start.1 = (f32[4,2,1,8192]{3,2,0,1:T(1,128)S(1)}, f32[4,2,1,8192]{3,2,0,1:T(1,128)S(1)}, u32[]{:S(2)}, u32[]{:S(2)}) collective-permute-start(f32[4,2,1,8192]{3,2,0,1:T(1,128)S(1)} %get-tuple-element.39), channel_id=1, source_target_pairs={{1,0},{2,1},{3,2},{4,3},{5,4},{6,5},{7,6},{8,7},{9,8},{10,9},{11,1... | collective-permute-start | bytes 786440 | tf_op jit(solution)/shard_map/ppermute | solution.py:20
  261.1 23.8 %all-to-all-start.1 = ((bf16[384,2,512]{2,1,0:T(2,128)(2,1)}), bf16[384,2,512]{2,1,0:T(2,128)(2,1)S(1)}, u32[]{:S(2)}, u32[]{:S(2)}) async-start(bf16[384,2,512]{2,1,0:T(2,128)(2,1)} %convert_element_type.86), calls=%async_computation.1 | async-start | bytes 1572864 | tf_op jit(solution)/shard_map/all_to_all | solution.py:187
Sparse Core Ops, SparseCore 0:
  203.2 43.2 all-reduce.3
where the time goes:
time: 294 us; the launch traced here: 293 us
  local copies, waits for them, and re-layouts  124 us (42%)
  waiting for transfers between devices  62.4 us (21%)
  matrix products  46.2 us (16%)
  starting transfers between devices  24.6 us (8%)
  other arithmetic  21.1 us (7%)
  between operations  14.4 us (5%)
    reshape x1, local copies, waits for them, and re-layouts, local(): received.reshape(row_count, degree_count, time_count, 2, 2)  53.4 us
    psum x1, waiting for transfers between devices, local(): lax.psum(okubo_weiss.astype(jnp.bfloat16), 'lev').astype(jnp.float32)  43.4 us
    gather x2, local copies, waits for them, and re-layouts, longitude_synthesis(): ordered = jnp.take(coeffs, slot_of_wave, axis=1).astype(jnp.float32)  36.9 us
    all_to_all x1, waiting for transfers between devices, local(): lax.all_to_all(outgoing.astype(jnp.bfloat16), 'band', split_axis=0, conca...  13.3 us
    dot_general x1, matrix products, local(): jnp.einsum('gtfcsn,shn->ghstfc', paired, legendre, preferred_element_type...  13 us
    all_to_all x1, starting transfers between devices, local(): lax.all_to_all(fourier, 'band', split_axis=0, concat_axis=1, tiled=True)  9.6 us
    all_to_all x1, starting transfers between devices, local(): lax.all_to_all(outgoing.astype(jnp.bfloat16), 'band', split_axis=0, conca...  9.52 us
    convert_element_type x1, other arithmetic, local(): even_input = scaled.astype(jnp.bfloat16)  8.81 us
  transfers between devices with their start and end apart: 5, of which 4 were waited for; matrix products, arithmetic and copies ran while one was open for 4% of the time, Pallas kernels for 0%

commit v1 on v0

v1 whole, which is shorter than its diff:
```python
import math

import jax
import jax.numpy as jnp
import ml_dtypes
import numpy as np
from jax import lax
from jax.experimental import pallas as pl
from jax.experimental.pallas import tpu as pltpu
from jax.sharding import PartitionSpec as P

MESH = pl.DeviceIdType.MESH
F32 = jnp.float32
BF16 = jnp.bfloat16

BANDS = 32
LEVS = 4
SLOTS = 64
K = 2048
NLON = 8192
HALF = 64
TIMES = 4
GROUP = 16
WIDTH = 128
CANDS = 192
CAP = 12
ROUNDS = CAP // 4


def bf16_split(table):
    high = table.astype(np.float32).astype(ml_dtypes.bfloat16)
    low = (table - high.astype(np.float64)).astype(np.float32).astype(ml_dtypes.bfloat16)
    return high, low


def degree_table():
    n = np.arange(K, dtype=np.float32)
    inverse = np.where(n >= 1, np.float32(-1.0) / np.maximum(n * (n + 1), np.float32(1.0)), 0.0)
    table = np.zeros((8, K), np.float32)
    table[0] = inverse
    table[1] = np.where(np.arange(K) % 2 == 0, 1.0, -1.0)
    return table


def row_table():
    hy = math.pi / 4096.0
    j = np.arange(HALF)
    hx = np.cos((63.5 - j) * hy) * 2.0 * math.pi / NLON
    table = np.zeros((8, WIDTH), np.float64)
    table[0, :HALF] = table[0, HALF:] = 1.0 / (hx * hx)
    table[1, :HALF] = 1.0 / (4.0 * hx * hy)
    table[1, HALF:] = -1.0 / (4.0 * hx * hy)
    table[2] = 1.0 / (hy * hy)
    return table.astype(np.float32)


def first_table():
    h = np.arange(32)[:, None]
    x = np.arange(WIDTH)[None, :]
    angle = 2.0 * np.pi * ((h * x) % 128) / 128.0
    cos, sin = np.cos(angle), np.sin(angle)
    table = np.concatenate(
        [np.concatenate([cos, sin], 1), np.concatenate([-sin, cos], 1)], 0
    )
    high, low = bf16_split(table)
    return np.concatenate([high, low], 0)


def twiddle_table():
    low = np.arange(64)[:, None]
    x = np.arange(WIDTH)[None, :]
    angle = 2.0 * np.pi * (low * x) / NLON
    cos, sin = np.cos(angle), np.sin(angle)
    return np.stack([np.concatenate([cos, cos], 0), np.concatenate([sin, sin], 0)], 0).astype(
        np.float32
    )


def second_table():
    y = np.arange(64)[:, None]
    low = np.arange(64)[None, :]
    angle = 2.0 * np.pi * ((y * low) % 64) / 64.0
    cos, sin = np.cos(angle), -np.sin(angle)
    zero = np.zeros_like(cos)
    table = np.concatenate(
        [
            np.concatenate([cos, zero, sin, zero], 1),
            np.concatenate([zero, cos, zero, sin], 1),
        ],
        0,
    )
    high, low_part = bf16_split(table)
    return np.concatenate([high, low_part, high], 1)


ORDERS = ((0, 0), (1, 0), (0, 1), (2, 0), (1, 1), (0, 2), (3, 0), (2, 1), (1, 2), (0, 3))


def ortho_values(count):
    u = np.arange(count, dtype=np.float64) - (count - 1) / 2.0
    q = np.stack(
        [
            np.ones_like(u),
            u,
            u * u - (count * count - 1) / 12.0,
            u * u * u - (3 * count * count - 7) / 20.0 * u,
        ],
        0,
    )
    return q / np.sqrt(np.sum(q * q, 1, keepdims=True))


def fit_tables():
    across, upward = ortho_values(WIDTH), ortho_values(4)
    columns = np.stack([across[a] for a, _ in ORDERS], 1)
    table = np.zeros((256, 32), np.float64)
    table[:128, 0:10] = columns
    table[128:, 10:20] = columns
    high, low = bf16_split(table)
    both = np.zeros((256, 128), high.dtype)
    both[:, 0:32] = high
    both[:, 32:64] = low
    rows = np.zeros((8, 128), np.float32)
    for r in range(4):
        line = [upward[b][r] / 4.0 for _, b in ORDERS]
        rows[r, 0:10] = line
        rows[r, 10:20] = line
    return both, rows


def column_of(row):
    return jnp.broadcast_to(row, (WIDTH, WIDTH)).T


def legendre_kernel(
    spec_hbm,
    leg_hbm,
    wave_ref,
    degree_ref,
    rows_ref,
    recv,
    spec,
    leg,
    scaled,
    factor,
    columns,
    sums,
    turned,
    send,
    spec_sem,
    leg_sem,
    own_sem,
    send_sem,
    recv_sem,
):
    me = lax.axis_index("band")
    groups = SLOTS // GROUP

    def spec_copy(g):
        window = pl.ds(g * GROUP, GROUP)
        return pltpu.make_async_copy(
            spec_hbm.at[:, window, :], spec.at[:, window, :], spec_sem.at[g]
        )

    def leg_copy(g):
        window = pl.ds(g * GROUP, GROUP)
        return pltpu.make_async_copy(leg_hbm.at[window], leg.at[window], leg_sem.at[g])

    for g in range(groups):
        spec_copy(g).start()
        leg_copy(g).start()

    barrier = pltpu.get_barrier_semaphore()

    def greet(k, carry):
        pl.semaphore_signal(
            barrier,
            inc=1,
            device_id={"band": lax.rem(me + k, BANDS)},
            device_id_type=MESH,
        )
        return carry

    lax.fori_loop(1, BANDS, greet, 0)

    line = wave_ref[pl.ds(me // 2, 1), :].astype(F32)
    columns[...] = column_of(line)
    first = pl.multiple_of(lax.rem(me, 2) * SLOTS, SLOTS)
    lane = lax.broadcasted_iota(jnp.int32, (1, K), 1).astype(F32)

    def one_group(g, carry):
        spec_copy(g).wait()
        own = columns[pl.ds(pl.multiple_of(first + g * GROUP, GROUP), GROUP), :]
        own = jnp.concatenate([own] * (K // WIDTH), axis=1)
        factor[...] = jnp.where(lane >= own, degree_ref[0:1, :], 0.0)
        start = pl.multiple_of(g * GROUP, GROUP)

        def scale(q, inner):
            part = spec[q, pl.ds(start, GROUP), :].astype(F32) * factor[...]
            window = pl.ds(pl.multiple_of(q * GROUP, GROUP), GROUP)
            for tile in range(K // WIDTH):
                scaled[tile, window, :] = part[:, tile * WIDTH : (tile + 1) * WIDTH]
            return inner

        lax.fori_loop(0, 16, scale, 0)
        leg_copy(g).wait()

        def one_slot(i, inner):
            even = jnp.concatenate(
                [scaled[tile, pl.ds(i, 16, stride=GROUP), :] for tile in range(K // WIDTH)],
                axis=1,
            )
            odd = even * degree_ref[1:2, :]
            both = jnp.concatenate([even.astype(BF16), odd.astype(BF16)], axis=0)
            result = lax.dot_general(
                both,
                leg[start + i],
                (((1,), (1,)), ((), ())),
                preferred_element_type=F32,
            )
            result = result.astype(BF16).astype(F32)
            sums[pl.ds(pl.multiple_of((start + i) * 16, 16), 16), :] = jnp.concatenate(
                [result[:16], result[16:]], axis=1
            )
            return inner

        lax.fori_loop(0, GROUP, one_slot, 0)
        return carry

    lax.fori_loop(0, groups, one_group, 0)

    m = columns[pl.ds(first, SLOTS), :]
    lanes = lax.broadcasted_iota(jnp.int32, (SLOTS, WIDTH), 1)
    half_m = jnp.floor(m * 0.5)
    parity = 1.0 - 2.0 * (m - 2.0 * half_m)
    weight = jnp.where(m == 0.0, 1.0, 2.0)
    sign = jnp.where(lanes >= HALF, parity, 1.0) * weight
    x = m * (math.pi / NLON)
    x2 = x * x
    sin = x * (
        1.0
        + x2 * (-1.0 / 6 + x2 * (1.0 / 120 + x2 * (-1.0 / 5040 + x2 * (1.0 / 362880))))
    )
    cos = 1.0 + x2 * (
        -0.5
        + x2 * (1.0 / 24 + x2 * (-1.0 / 720 + x2 * (1.0 / 40320 - x2 * (1.0 / 3628800))))
    )
    xx = -4.0 * sin * sin * rows_ref[0:1, :]
    xy = 2.0 * (2.0 * sin * cos) * rows_ref[1:2, :]
    yy = rows_ref[2:3, :]
    first_lane = (lanes == 0) | (lanes == HALF)
    last_lane = (lanes == HALF - 1) | (lanes == WIDTH - 1)

    def one_time(t, carry):
        def pieces(q):
            c = sums[pl.ds(t * 4 + q, SLOTS, stride=16), :] * sign
            before = jnp.where(first_lane, 0.0, pltpu.roll(c, 1, 1))
            after = jnp.where(last_lane, pltpu.roll(c, HALF, 1), pltpu.roll(c, WIDTH - 1, 1))
            return c * xx, (before + after - 2.0 * c) * yy, (before - after) * xy

        pr_xx, pr_yy, pr_xy = pieces(0)
        pi_xx, pi_yy, pi_xy = pieces(1)
        cr_xx, cr_yy, cr_xy = pieces(2)
        ci_xx, ci_yy, ci_xy = pieces(3)
        vort = (pr_xx + pr_yy, pi_xx + pi_yy)
        normal = (2.0 * pi_xy + cr_xx - cr_yy, -2.0 * pr_xy + ci_xx - ci_yy)
        shear = (pr_xx - pr_yy - 2.0 * ci_xy, pi_xx - pi_yy + 2.0 * cr_xy)
        for q, pair in enumerate((vort, normal, shear)):
            block = jnp.concatenate(pair, axis=0).T
            turned[q, pl.ds(t, WIDTH, stride=4), :] = block
        return carry

    lax.fori_loop(0, TIMES, one_time, 0)

    pl.semaphore_wait(barrier, BANDS - 1)

    def place(d):
        return jnp.where(d < BANDS // 2, d, BANDS + BANDS // 2 - 1 - d)

    def message(k):
        d = lax.rem(me + k, BANDS)
        return pltpu.make_async_remote_copy(
            src_ref=send.at[k],
            dst_ref=recv.at[me],
            send_sem=send_sem.at[k],
            recv_sem=recv_sem.at[me],
            device_id={"band": d},
            device_id_type=MESH,
        )

    def fill(k):
        p = place(lax.rem(me + k, BANDS))
        for q in range(3):
            send[k, 16 * q : 16 * q + 16, :] = turned[
                q, pl.ds(pl.multiple_of(p * 16, 16), 16), :
            ].astype(BF16)

    def post(k, carry):
        fill(k)
        message(k).start()
        return carry

    lax.fori_loop(1, BANDS, post, 0)
    fill(0)
    own_copy = pltpu.make_async_copy(send.at[0], recv.at[me], own_sem)
    own_copy.start()

    def finish(k, carry):
        message(k).wait_send()
        source = lax.rem(me + k, BANDS)
        pltpu.make_async_remote_copy(
            src_ref=send.at[k],
            dst_ref=recv.at[source],
            send_sem=send_sem.at[k],
            recv_sem=recv_sem.at[source],
            device_id={"band": source},
            device_id_type=MESH,
        ).wait_recv()
        return carry

    lax.fori_loop(1, BANDS, finish, 0)
    own_copy.wait()


def legendre_part(spectra, legendre, waves):
    vmem = pl.BlockSpec(memory_space=pltpu.VMEM)
    hbm = pl.BlockSpec(memory_space=pl.ANY)
    return pl.pallas_call(
        legendre_kernel,
        out_shape=jax.ShapeDtypeStruct((BANDS, 48, WIDTH), BF16),
        in_specs=[hbm, hbm, vmem, vmem, vmem],
        out_specs=vmem,
        scratch_shapes=[
            pltpu.VMEM((16, SLOTS, K), BF16),
            pltpu.VMEM((SLOTS, HALF, K), BF16),
            pltpu.VMEM((K // WIDTH, 16 * GROUP, WIDTH), F32),
            pltpu.VMEM((GROUP, K), F32),
            pltpu.VMEM((WIDTH, WIDTH), F32),
            pltpu.VMEM((SLOTS * 16, WIDTH), F32),
            pltpu.VMEM((3, 4 * WIDTH, WIDTH), F32),
            pltpu.VMEM((BANDS, 48, WIDTH), BF16),
            pltpu.SemaphoreType.DMA((SLOTS // GROUP,)),
            pltpu.SemaphoreType.DMA((SLOTS // GROUP,)),
            pltpu.SemaphoreType.DMA,
            pltpu.SemaphoreType.DMA((BANDS,)),
            pltpu.SemaphoreType.DMA((BANDS,)),
        ],
        compiler_params=pltpu.CompilerParams(
            collective_id=0, has_side_effects=True, vmem_limit_bytes=56 * 1024 * 1024
        ),
        name="legendre_transpose",
    )(spectra, legendre, waves, degree_table(), row_table())


def grid_kernel(
    coeffs,
    wave_ref,
    owner_ref,
    block_ref,
    first_ref,
    twiddle_ref,
    second_ref,
    fit_ref,
    fit_rows,
    vort_out,
    okubo_out,
    picked_out,
    ordered_in,
    onehot,
    spread,
    table,
):
    band = lax.axis_index("band")
    lane = lax.broadcasted_iota(jnp.int32, (WIDTH, WIDTH), 1)
    low_lanes = lane < 64

    def one_block(j, carry):
        column = column_of(wave_ref[pl.ds(j, 1), :].astype(F32))
        rows = pl.ds(pl.multiple_of(j * WIDTH, WIDTH), WIDTH)
        for tile in range(K // WIDTH):
            wanted = lane.astype(F32) + float(tile * WIDTH)
            onehot[rows, tile * WIDTH : (tile + 1) * WIDTH] = jnp.where(
                column == wanted, 1.0, 0.0
            ).astype(BF16)
        return carry

    lax.fori_loop(0, K // WIDTH, one_block, 0)

    pick = low_lanes[:48]
    for j in range(BANDS // 2):
        a = coeffs[2 * j].astype(F32)
        b = coeffs[2 * j + 1].astype(F32)
        real = jnp.where(pick, a, pltpu.roll(b, 64, 1))
        imag = jnp.where(pick, pltpu.roll(a, 64, 1), b)
        ordered_in[0:48, j * WIDTH : (j + 1) * WIDTH] = real.astype(BF16)
        ordered_in[48:96, j * WIDTH : (j + 1) * WIDTH] = imag.astype(BF16)

    pick = low_lanes[:8]
    for j in range(8):
        part = jnp.dot(
            ordered_in[...], onehot[:, 256 * j : 256 * (j + 1)], preferred_element_type=F32
        )
        for tile in range(2):
            h = 4 * j + 2 * tile
            for c in range(2):
                for f in range(3):
                    at = c * 48 + f * 16
                    a = part[at : at + 8, tile * WIDTH : (tile + 1) * WIDTH]
                    b = part[at + 8 : at + 16, tile * WIDTH : (tile + 1) * WIDTH]
                    to = c * 24 + f * 8
                    spread[h * 48 + to : h * 48 + to + 8, :] = jnp.where(
                        pick, a, pltpu.roll(b, 64, 1)
                    )
                    spread[(h + 1) * 48 + to : (h + 1) * 48 + to + 8, :] = jnp.where(
                        pick, pltpu.roll(a, 64, 1), b
                    )

    southern = band >= BANDS // 2
    table[...] = jnp.zeros_like(table)
    for rr in range(2):
        row_low = jnp.where(southern, 3 - rr, rr)
        row_high = jnp.where(southern, 1 - rr, 2 + rr)

        def one_time(t, carry, rr=rr, row_low=row_low, row_high=row_high):
            parts = []
            for f in range(3):
                i = f * 8 + rr * 4 + t
                c = jnp.concatenate(
                    [spread[pl.ds(i, 32, stride=48), :], spread[pl.ds(24 + i, 32, stride=48), :]],
                    axis=0,
                ).T.astype(BF16)
                z = jnp.dot(
                    jnp.concatenate([c, c], axis=1), first_ref[...], preferred_element_type=F32
                )
                zr, zi = z[:, :WIDTH], z[:, WIDTH:]
                tc, ts = twiddle_ref[0], twiddle_ref[1]
                parts.append(jnp.concatenate([zr * tc - zi * ts, zr * ts + zi * tc], axis=0))
            z = jnp.concatenate(parts, axis=1)
            high = z.astype(BF16)
            low = (z - high.astype(F32)).astype(BF16)
            grid = jnp.dot(
                second_ref[...],
                jnp.concatenate([high, high, low], axis=0),
                preferred_element_type=F32,
            )
            vort = grid[:, :WIDTH]
            normal = grid[:, WIDTH : 2 * WIDTH]
            shear = grid[:, 2 * WIDTH :]
            okubo = normal * normal + shear * shear - vort * vort
            vort_out[t, pl.ds(row_low, 64, stride=4), :] = vort[:64]
            vort_out[t, pl.ds(row_high, 64, stride=4), :] = vort[64:]
            okubo_out[t, pl.ds(row_low, 64, stride=4), :] = okubo[:64]
            okubo_out[t, pl.ds(row_high, 64, stride=4), :] = okubo[64:]
            both = jnp.concatenate([vort, okubo], axis=1)
            high = both.astype(BF16)
            low = (both - high.astype(F32)).astype(BF16)
            from_high = jnp.dot(high, fit_ref[...], preferred_element_type=F32)
            from_low = jnp.dot(low, fit_ref[...], preferred_element_type=F32)
            fits = from_high + pltpu.roll(from_high, WIDTH - 32, 1) + from_low
            window = pl.ds(pl.multiple_of(t * 64, 64), 64)
            table[window, :] += (
                fits[:64] * fit_rows[pl.ds(row_low, 1), :]
                + fits[64:] * fit_rows[pl.ds(row_high, 1), :]
            )
            return carry

        lax.fori_loop(0, TIMES, one_time, 0)

    lanes = lax.broadcasted_iota(jnp.int32, (CANDS, WIDTH), 1)
    owner = owner_ref[...]
    owned = jnp.where(owner == lanes, 1.0, 0.0)
    order = jnp.where(
        lax.broadcasted_iota(jnp.int32, (CANDS, CANDS), 1)
        < lax.broadcasted_iota(jnp.int32, (CANDS, CANDS), 0),
        1.0,
        0.0,
    ).astype(BF16)
    earlier = jnp.dot(order, owned.astype(BF16), preferred_element_type=F32)
    slot = jnp.sum(earlier * owned, axis=1, keepdims=True).astype(jnp.int32)
    target = (slot & 3) * WIDTH + owner * 4 + (slot >> 2)
    goal = jnp.where(
        lax.broadcasted_iota(jnp.int32, (CANDS, 4 * WIDTH), 1) == target, 1.0, 0.0
    )
    named = jnp.where(
        lax.broadcasted_iota(jnp.int32, (256, CANDS), 0) == block_ref[...], 1.0, 0.0
    )
    values = table[...]
    high = values.astype(BF16).astype(F32)
    low = values - high
    chosen = jnp.dot(
        named.T.astype(BF16),
        jnp.concatenate([high, low], axis=1).astype(BF16),
        preferred_element_type=F32,
    )
    total = jnp.zeros((WIDTH, WIDTH), F32)
    for g in range(4):
        high = chosen[:, :WIDTH]
        low = chosen[:, WIDTH:]
        if g:
            high = pltpu.roll(high, 32 * g, 1)
            low = pltpu.roll(low, 32 * g, 1)
        which = goal[:, g * WIDTH : (g + 1) * WIDTH].T.astype(BF16)
        total += jnp.dot(which, high.astype(BF16), preferred_element_type=F32)
        total += jnp.dot(which, low.astype(BF16), preferred_element_type=F32)
    picked_out[...] = total


def grid_part(coeffs, waves, owner, block):
    vmem = pl.BlockSpec(memory_space=pltpu.VMEM)
    fit_table, fit_rows = fit_tables()
    return pl.pallas_call(
        grid_kernel,
        out_shape=(
            jax.ShapeDtypeStruct((TIMES, 256, WIDTH), F32),
            jax.ShapeDtypeStruct((TIMES, 256, WIDTH), F32),
            jax.ShapeDtypeStruct((WIDTH, WIDTH), F32),
        ),
        in_specs=[vmem] * 9,
        out_specs=(vmem, vmem, vmem),
        scratch_shapes=[
            pltpu.VMEM((96, K), BF16),
            pltpu.VMEM((K, K), BF16),
            pltpu.VMEM((32 * 48, WIDTH), F32),
            pltpu.VMEM((256, WIDTH), F32),
        ],
        compiler_params=pltpu.CompilerParams(vmem_limit_bytes=48 * 1024 * 1024),
        name="grid_synthesis",
    )(
        coeffs,
        waves,
        owner,
        block,
        first_table(),
        twiddle_table(),
        second_table(),
        fit_table,
        fit_rows,
    )


def owner_kernel(mine, fits_out, parts, summed, arrived, own_sem, send_a, recv_a, send_b, recv_b):
    lev = lax.axis_index("lev")
    band = lax.axis_index("band")
    group = band // 8
    inside = group == lev

    barrier = pltpu.get_barrier_semaphore()
    for k in range(1, LEVS):
        pl.semaphore_signal(
            barrier,
            inc=1,
            device_id={"lev": lax.rem(lev + k, LEVS), "band": band},
            device_id_type=MESH,
        )

    def greet(k, carry):
        source = lax.rem(band + k, BANDS)

        @pl.when(jnp.logical_not(inside & (k == 0)))
        def _():
            pl.semaphore_signal(
                barrier,
                inc=1,
                device_id={"lev": group, "band": source},
                device_id_type=MESH,
            )

        return carry

    lax.fori_loop(0, BANDS, greet, 0)
    pl.semaphore_wait(barrier, LEVS - 1 + BANDS - inside.astype(jnp.int32))

    def level_copy(k):
        to = lax.rem(lev + k, LEVS)
        return pltpu.make_async_remote_copy(
            src_ref=mine.at[pl.ds(to * 8, 8)],
            dst_ref=parts.at[lev],
            send_sem=send_a.at[k],
            recv_sem=recv_a.at[lev],
            device_id={"lev": to, "band": band},
            device_id_type=MESH,
        )

    for k in range(1, LEVS):
        level_copy(k).start()
    parts[lev] = mine[pl.ds(lev * 8, 8)]
    for k in range(1, LEVS):
        source = lax.rem(lev + k, LEVS)
        pltpu.make_async_remote_copy(
            src_ref=mine.at[pl.ds(source * 8, 8)],
            dst_ref=parts.at[source],
            send_sem=send_a.at[k],
            recv_sem=recv_a.at[source],
            device_id={"lev": source, "band": band},
            device_id_type=MESH,
        ).wait_recv()
    summed[...] = (parts[0] + parts[1]) + (parts[2] + parts[3])

    def owner_copy(k):
        to = lax.rem(lev + k // 8, LEVS)
        o = lax.rem(band + k, 8)
        return (
            jnp.logical_not((to == lev) & (lev * 8 + o == band)),
            o,
            pltpu.make_async_remote_copy(
                src_ref=summed.at[o],
                dst_ref=arrived.at[band],
                send_sem=send_b.at[k],
                recv_sem=recv_b.at[band],
                device_id={"lev": to, "band": lev * 8 + o},
                device_id_type=MESH,
            ),
        )

    def post(k, carry):
        other, o, copy = owner_copy(k)

        @pl.when(other)
        def _():
            copy.start()

        @pl.when(jnp.logical_not(other))
        def _():
            pltpu.make_async_copy(summed.at[o], arrived.at[band], own_sem).start()

        return carry

    lax.fori_loop(0, BANDS, post, 0)

    def finish(k, carry):
        other, o, copy = owner_copy(k)

        @pl.when(other)
        def _():
            copy.wait_send()

        @pl.when(jnp.logical_not(other))
        def _():
            pltpu.make_async_copy(summed.at[o], arrived.at[band], own_sem).wait()

        source = lax.rem(band + k, BANDS)

        @pl.when(jnp.logical_not(inside & (k == 0)))
        def _():
            pltpu.make_async_remote_copy(
                src_ref=summed.at[o],
                dst_ref=arrived.at[source],
                send_sem=send_b.at[k],
                recv_sem=recv_b.at[source],
                device_id={"lev": group, "band": source},
                device_id_type=MESH,
            ).wait_recv()

        return carry

    lax.fori_loop(0, BANDS, finish, 0)
    for k in range(1, LEVS):
        level_copy(k).wait_send()

    for r in range(ROUNDS):
        line = arrived[:, r, :]
        for g in range(4):
            value = pltpu.roll(line, WIDTH - 32 * g, 1) if g else line
            fits_out[pl.ds(4 * r + g, BANDS, stride=CAP), :] = value


def owner_part(picked):
    vmem = pl.BlockSpec(memory_space=pltpu.VMEM)
    return pl.pallas_call(
        owner_kernel,
        out_shape=jax.ShapeDtypeStruct((BANDS * CAP, WIDTH), F32),
        in_specs=[vmem],
        out_specs=vmem,
        scratch_shapes=[
            pltpu.VMEM((LEVS, 8, 4, WIDTH), F32),
            pltpu.VMEM((8, 4, WIDTH), F32),
            pltpu.VMEM((BANDS, 4, WIDTH), F32),
            pltpu.SemaphoreType.DMA,
            pltpu.SemaphoreType.DMA((LEVS,)),
            pltpu.SemaphoreType.DMA((LEVS,)),
            pltpu.SemaphoreType.DMA((BANDS,)),
            pltpu.SemaphoreType.DMA((BANDS,)),
        ],
        compiler_params=pltpu.CompilerParams(
            collective_id=1, has_side_effects=True, vmem_limit_bytes=16 * 1024 * 1024
        ),
        name="owner_exchange",
    )(picked)


def local(spectra, legendre, wave_order, cand_block, cand_owner):
    waves = wave_order.reshape(K // WIDTH, WIDTH)
    coeffs = legendre_part(spectra.reshape(16, SLOTS, K), legendre, waves)
    vort, okubo, picked = grid_part(coeffs, waves, cand_owner, cand_block.reshape(1, CANDS))
    fits = owner_part(picked.reshape(BANDS, 4, WIDTH))[:, :20]

    def rows(field):
        shaped = field.reshape(TIMES, 64, 4, WIDTH).transpose(0, 2, 1, 3)
        return shaped.reshape(1, TIMES, 4, NLON)

    return rows(vort), rows(okubo), fits


def solution(mesh):
    placed = (
        P("lev", None, None, None, "band", None),
        P("band", None, None),
        P(),
        P("band"),
        P("band", None),
    )
    return jax.shard_map(
        local,
        mesh=mesh,
        in_specs=placed,
        out_specs=(P("lev", None, "band", None), P("lev", None, "band", None), P("band", None)),
        check_vma=False,
    )
```

time: 294 us -> 68 us (0.23)
  local copies, waits for them, and re-layouts: 124 us -> 2.65 us
  Pallas kernels: 0 us -> 64.4 us
  waiting for transfers between devices: 62.4 us -> 0 us
  matrix products: 46.2 us -> 0 us
  starting transfers between devices: 24.6 us -> 0 us
  other arithmetic: 21.1 us -> 0 us
  between operations: 14.4 us -> 0.77 us
    pallas_call x0 -> x3, Pallas kernels: none -> 64.4 us  [the longest x1 37.4 us: legendre_part(): pl.pallas_call(legendre_kernel, out_shape=jax.ShapeDtypeStruct((BANDS, 48...]
    reshape x5 -> x0, local copies, waits for them, and re-layouts: 55.7 us -> none  [the longest x1 53.4 us: local(): received.reshape(row_count, degree_count, time_count, 2, 2)]
    dot_general x8 -> x0, matrix products: 46.2 us -> none  [the longest x1 13 us: local(): jnp.einsum('gtfcsn,shn->ghstfc', paired, legendre, preferred_element_type...]
    psum x1 -> x0, waiting for transfers between devices: 43.4 us -> none  [local(): lax.psum(okubo_weiss.astype(jnp.bfloat16), 'lev').astype(jnp.float32)]
    gather x3 -> x0, local copies, waits for them, and re-layouts: 39.2 us -> none  [the longest x2 36.9 us: longitude_synthesis(): ordered = jnp.take(coeffs, slot_of_wave, axis=1).astype(jnp.float32)]
    all_to_all x2 -> x0, starting transfers between devices: 19.1 us -> none  [the longest x1 9.6 us: local(): lax.all_to_all(fourier, 'band', split_axis=0, concat_axis=1, tiled=True)]
    scatter x2 -> x0, local copies, waits for them, and re-layouts: 14.4 us -> none  [the longest x1 8.23 us: longitude_synthesis(): slot_of_wave = jnp.zeros((slot_total,), jnp.int32).at[wave_order].set(jnp...]
    all_to_all x2 -> x0, waiting for transfers between devices: 13.3 us -> none  [the longest x1 13.3 us: local(): lax.all_to_all(outgoing.astype(jnp.bfloat16), 'band', split_axis=0, conca...]
  transfers between devices with their start and end apart: 5 -> 0, of which waited for: 4 -> 0; matrix products, arithmetic and copies ran while one was open for 4% -> 0% of each run, Pallas kernels for 0% -> 0%
where the time goes in v1:
time: 68 us; the launch traced here: 67.8 us
  Pallas kernels  64.4 us (95%)
  local copies, waits for them, and re-layouts  2.65 us (4%)
  between operations  0.77 us (1%)
    pallas_call x1, Pallas kernels, legendre_part(): pl.pallas_call(legendre_kernel, out_shape=jax.ShapeDtypeStruct((BANDS, 48...  37.4 us
    pallas_call x1, Pallas kernels, owner_part(): pl.pallas_call(owner_kernel, out_shape=jax.ShapeDtypeStruct((BANDS * CAP,...  14.3 us
    pallas_call x1, Pallas kernels, grid_part(): pl.pallas_call(grid_kernel, out_shape=(jax.ShapeDtypeStruct((TIMES, 256,...  12.6 us
    unnamed x18, local copies, waits for them, and re-layouts  2.65 us

profile of v1, /device:TPU:1, one launch (start us, length us, event | category | flops | bytes accessed | tf_op | source)
XLA Modules:
  0.0 67.8 jit_solution(5140000068183122530)
XLA Ops:
  0.6 0.0 copy-start.6
  0.6 0.0 copy-start.3
  0.7 0.0 copy-start.1
  0.7 0.0 copy-start.2
  0.7 0.0 copy-start.4
  0.7 0.0 copy-start.7
  0.7 0.0 copy-start.5
  0.7 0.9 %copy.15.owner_ref = s32[192,1]{1,0:T(8,128)S(1)} copy(s32[192,1]{0,1:T(1,128)} %param.16) | data formatting | bytes 1536 | tf_op args[4]
  1.6 37.4 %legendre_transpose.1.coeffs = bf16[32,48,128]{2,1,0:T(8,128)(2,1)} custom-call(bf16[16,64,2048]{2,1,0:T(8,128)(2,1)} %bitcast.20, bf16[64,64,2048]{2,1,0:T(8,128)(2,1)} %leg_hbm.1, s32[16,128]{1,0:T(8,128)} %bitcast.17, f32[8,2048]{1,0:T(8,128)} %constant.14.clone.degree_ref, f32[8,128]{1,0:T(8,128)} %constant.15.clone.rows_ref), custom_call_target="tpu_custom_call" | custom-call | tf_op jit(solution)/shard_map/legendre_transpose/pallas_call | solution.py:328
  39.0 0.0 copy-done.6
  39.1 0.0 copy-done.3
  39.1 0.0 copy-done.1
  39.1 0.0 copy-done.2
  39.1 0.0 copy-done.4
  39.1 0.0 copy-done.7
  39.1 0.0 copy-done.5
  39.1 0.0 copy-start
  39.1 1.0 %copy-done = bf16[32,48,128]{2,1,0:T(8,128)(2,1)S(1)} copy-done((bf16[32,48,128]{2,1,0:T(8,128)(2,1)S(1)}, bf16[32,48,128]{2,1,0:T(8,128)(2,1)}, u32[]{:S(2)}) %copy-start) | copy-done | bytes 393240
  40.1 12.6 %grid_synthesis.1 = (f32[4,256,128]{2,1,0:T(8,128)}, f32[4,256,128]{2,1,0:T(8,128)}, f32[128,128]{1,0:T(8,128)S(1)}) custom-call(bf16[32,48,128]{2,1,0:T(8,128)(2,1)S(1)} %copy-done, s32[16,128]{1,0:T(8,128)S(1)} %bitcast.18, s32[192,1]{1,0:T(8,128)S(1)} %copy.15.owner_ref, s32[1,192]{1,0:T(1,128)S(1)} %bitcast.19, bf16[128,256]{1,0:T(8,128)(2,1)S(1)} %copy-done.4, ...), custom_call_target="tpu_custom_call" | custom-call | tf_op jit(solution)/shard_map/grid_synthesis/pallas_call | solution.py:511
  52.8 14.3 %owner_exchange.1 = f32[384,128]{1,0:T(8,128)S(1)} custom-call(f32[32,4,128]{2,1,0:T(4,128)S(1)} %bitcast.16), custom_call_target="tpu_custom_call" | custom-call | tf_op jit(solution)/shard_map/owner_exchange/pallas_call | solution.py:669
  67.1 0.7 %copy.18 = f32[384,20]{0,1:T(8,128)} copy(f32[384,20]{1,0:T(8,128)S(1)} %bitcast.15) | data formatting | bytes 61440
Async XLA Ops:
  0.6 38.4 %copy-start.6 = (f32[8,128]{1,0:T(8,128)S(1)}, f32[8,128]{1,0:T(8,128)}, u32[]{:S(2)}) copy-start(f32[8,128]{1,0:T(8,128)} %constant.20.clone.fit_rows) | copy-start | bytes 12292
  0.6 38.4 %copy-start.3 = (bf16[256,128]{1,0:T(8,128)(2,1)S(1)}, bf16[256,128]{1,0:T(8,128)(2,1)}, u32[]{:S(2)}) copy-start(bf16[256,128]{1,0:T(8,128)(2,1)} %constant.19.clone.fit_ref) | copy-start | bytes 196612
  0.7 38.4 %copy-start.1 = (bf16[128,768]{1,0:T(8,128)(2,1)S(1)}, bf16[128,768]{1,0:T(8,128)(2,1)}, u32[]{:S(2)}) copy-start(bf16[128,768]{1,0:T(8,128)(2,1)} %constant.18.clone.second_ref) | copy-start | bytes 589828
  0.7 38.4 %copy-start.2 = (f32[2,128,128]{2,1,0:T(8,128)S(1)}, f32[2,128,128]{2,1,0:T(8,128)}, u32[]{:S(2)}) copy-start(f32[2,128,128]{2,1,0:T(8,128)} %constant.17.clone.twiddle_ref) | copy-start | bytes 393220
  0.7 38.4 %copy-start.4 = (bf16[128,256]{1,0:T(8,128)(2,1)S(1)}, bf16[128,256]{1,0:T(8,128)(2,1)}, u32[]{:S(2)}) copy-start(bf16[128,256]{1,0:T(8,128)(2,1)} %constant.16.clone.first_ref) | copy-start | bytes 196612
  0.7 38.4 %copy-start.7 = (s32[192]{0:T(256)S(1)}, s32[192]{0:T(256)}, u32[]{:S(2)}) copy-start(s32[192]{0:T(256)} %param.15) | copy-start | bytes 2308
  0.7 38.4 %copy-start.5 = (s32[2048]{0:T(1024)S(1)}, s32[2048]{0:T(1024)}, u32[]{:S(2)}) copy-start(s32[2048]{0:T(1024)} %param.14) | copy-start | bytes 24580
  39.1 1.0 %copy-start = (bf16[32,48,128]{2,1,0:T(8,128)(2,1)S(1)}, bf16[32,48,128]{2,1,0:T(8,128)(2,1)}, u32[]{:S(2)}) copy-start(bf16[32,48,128]{2,1,0:T(8,128)(2,1)} %legendre_transpose.1.coeffs) | copy-start | bytes 1179652

commit v2 on v1

v2 whole, which is shorter than its diff:
```python
import math

import jax
import jax.numpy as jnp
import ml_dtypes
import numpy as np
from jax import lax
from jax.experimental import pallas as pl
from jax.experimental.pallas import tpu as pltpu
from jax.sharding import PartitionSpec as P

MESH = pl.DeviceIdType.MESH
F32 = jnp.float32
BF16 = jnp.bfloat16

BANDS = 32
LEVS = 4
SLOTS = 64
K = 2048
NLON = 8192
HALF = 64
TIMES = 4
GROUP = 16
PLANE = 8
PLANES = 4
MEMBERS = 128
WIDTH = 128
CANDS = 192
CAP = 12
ROUNDS = CAP // 4


def bf16_split(table):
    high = table.astype(np.float32).astype(ml_dtypes.bfloat16)
    low = (table - high.astype(np.float64)).astype(np.float32).astype(ml_dtypes.bfloat16)
    return high, low


def degree_table():
    n = np.arange(K, dtype=np.float32)
    inverse = np.where(n >= 1, np.float32(-1.0) / np.maximum(n * (n + 1), np.float32(1.0)), 0.0)
    table = np.zeros((8, K), np.float32)
    table[0] = inverse
    table[1] = np.where(np.arange(K) % 2 == 0, 1.0, -1.0)
    return table


def row_table():
    hy = math.pi / 4096.0
    j = np.arange(HALF)
    hx = np.cos((63.5 - j) * hy) * 2.0 * math.pi / NLON
    table = np.zeros((8, WIDTH), np.float64)
    table[0, :HALF] = table[0, HALF:] = 1.0 / (hx * hx)
    table[1, :HALF] = 1.0 / (4.0 * hx * hy)
    table[1, HALF:] = -1.0 / (4.0 * hx * hy)
    table[2] = 1.0 / (hy * hy)
    return table.astype(np.float32)


def first_table():
    h = np.arange(32)[:, None]
    x = np.arange(WIDTH)[None, :]
    angle = 2.0 * np.pi * ((h * x) % 128) / 128.0
    cos, sin = np.cos(angle), np.sin(angle)
    table = np.concatenate(
        [np.concatenate([cos, sin], 1), np.concatenate([-sin, cos], 1)], 0
    )
    high, low = bf16_split(table)
    return np.concatenate([high, low], 0)


def twiddle_table():
    low = np.arange(64)[:, None]
    x = np.arange(WIDTH)[None, :]
    angle = 2.0 * np.pi * (low * x) / NLON
    cos, sin = np.cos(angle), np.sin(angle)
    return np.stack([np.concatenate([cos, cos], 0), np.concatenate([sin, sin], 0)], 0).astype(
        np.float32
    )


def second_table():
    y = np.arange(64)[:, None]
    low = np.arange(64)[None, :]
    angle = 2.0 * np.pi * ((y * low) % 64) / 64.0
    cos, sin = np.cos(angle), -np.sin(angle)
    zero = np.zeros_like(cos)
    table = np.concatenate(
        [
            np.concatenate([cos, zero, sin, zero], 1),
            np.concatenate([zero, cos, zero, sin], 1),
        ],
        0,
    )
    high, low_part = bf16_split(table)
    return np.concatenate([high, low_part, high], 1)


ORDERS = ((0, 0), (1, 0), (0, 1), (2, 0), (1, 1), (0, 2), (3, 0), (2, 1), (1, 2), (0, 3))


def ortho_values(count):
    u = np.arange(count, dtype=np.float64) - (count - 1) / 2.0
    q = np.stack(
        [
            np.ones_like(u),
            u,
            u * u - (count * count - 1) / 12.0,
            u * u * u - (3 * count * count - 7) / 20.0 * u,
        ],
        0,
    )
    return q / np.sqrt(np.sum(q * q, 1, keepdims=True))


def fit_tables():
    across, upward = ortho_values(WIDTH), ortho_values(4)
    columns = np.stack([across[a] for a, _ in ORDERS], 1)
    table = np.zeros((256, 32), np.float64)
    table[:128, 0:10] = columns
    table[128:, 10:20] = columns
    high, low = bf16_split(table)
    both = np.zeros((256, 128), high.dtype)
    both[:, 0:32] = high
    both[:, 32:64] = low
    rows = np.zeros((8, 128), np.float32)
    for r in range(4):
        line = [upward[b][r] / 4.0 for _, b in ORDERS]
        rows[r, 0:10] = line
        rows[r, 10:20] = line
    return both, rows


def column_of(row):
    return jnp.broadcast_to(row, (WIDTH, WIDTH)).T


def greet_all(barrier, rank):
    def greet(k, carry):
        other = lax.rem(rank + k, MEMBERS)
        pl.semaphore_signal(
            barrier,
            inc=1,
            device_id={"lev": other // BANDS, "band": lax.rem(other, BANDS)},
            device_id_type=MESH,
        )
        return carry

    lax.fori_loop(1, MEMBERS, greet, 0)


def legendre_sums(first, waits, spec, leg, degree_ref, columns, scaled, factor, sums):
    spec_wait, leg_wait = waits
    lane = lax.broadcasted_iota(jnp.int32, (1, K), 1).astype(F32)

    def one_group(g, carry):
        spec_wait(g)
        start = pl.multiple_of(g * GROUP, GROUP)
        own = columns[pl.ds(pl.multiple_of(first + start, GROUP), GROUP), :]
        own = jnp.concatenate([own] * (K // WIDTH), axis=1)
        factor[...] = jnp.where(lane >= own, degree_ref[0:1, :], 0.0)

        def scale(q, inner):
            part = spec[q, pl.ds(start, GROUP), :].astype(F32) * factor[...]
            window = pl.ds(pl.multiple_of(q * GROUP, GROUP), GROUP)
            for tile in range(K // WIDTH):
                scaled[tile, window, :] = part[:, tile * WIDTH : (tile + 1) * WIDTH]
            return inner

        lax.fori_loop(0, 16, scale, 0)

        def one_slot(i, inner):
            even = jnp.concatenate(
                [scaled[tile, pl.ds(i, 16, stride=GROUP), :] for tile in range(K // WIDTH)],
                axis=1,
            )
            odd = even * degree_ref[1:2, :]
            both = jnp.concatenate([even.astype(BF16), odd.astype(BF16)], axis=0)
            result = lax.dot_general(
                both,
                leg[start + i],
                (((1,), (1,)), ((), ())),
                preferred_element_type=F32,
            )
            result = result.astype(BF16).astype(F32)
            sums[pl.ds(pl.multiple_of((start + i) * 16, 16), 16), :] = jnp.concatenate(
                [result[:16], result[16:]], axis=1
            )
            return inner

        for part in range(GROUP // LEG_PART):
            leg_wait(g * (GROUP // LEG_PART) + part)
            lax.fori_loop(
                part * LEG_PART, (part + 1) * LEG_PART, one_slot, 0, unroll=LEG_PART
            )
        return carry

    lax.fori_loop(0, SLOTS // GROUP, one_group, 0)


LEG_PART = 8


def combine_rows(first, columns, rows_ref, sums, turned):
    m = columns[pl.ds(first, SLOTS), :]
    lanes = lax.broadcasted_iota(jnp.int32, (SLOTS, WIDTH), 1)
    half_m = jnp.floor(m * 0.5)
    parity = 1.0 - 2.0 * (m - 2.0 * half_m)
    weight = jnp.where(m == 0.0, 1.0, 2.0)
    sign = jnp.where(lanes >= HALF, parity, 1.0) * weight
    x = m * (math.pi / NLON)
    x2 = x * x
    sin = x * (
        1.0
        + x2 * (-1.0 / 6 + x2 * (1.0 / 120 + x2 * (-1.0 / 5040 + x2 * (1.0 / 362880))))
    )
    cos = 1.0 + x2 * (
        -0.5
        + x2 * (1.0 / 24 + x2 * (-1.0 / 720 + x2 * (1.0 / 40320 - x2 * (1.0 / 3628800))))
    )
    xx = -4.0 * sin * sin * rows_ref[0:1, :]
    xy = 2.0 * (2.0 * sin * cos) * rows_ref[1:2, :]
    yy = rows_ref[2:3, :]
    first_lane = (lanes == 0) | (lanes == HALF)
    last_lane = (lanes == HALF - 1) | (lanes == WIDTH - 1)

    def one_time(t, carry):
        def pieces(q):
            c = sums[pl.ds(t * 4 + q, SLOTS, stride=16), :] * sign
            before = jnp.where(first_lane, 0.0, pltpu.roll(c, 1, 1))
            after = jnp.where(last_lane, pltpu.roll(c, HALF, 1), pltpu.roll(c, WIDTH - 1, 1))
            return c * xx, (before + after - 2.0 * c) * yy, (before - after) * xy

        pr_xx, pr_yy, pr_xy = pieces(0)
        pi_xx, pi_yy, pi_xy = pieces(1)
        cr_xx, cr_yy, cr_xy = pieces(2)
        ci_xx, ci_yy, ci_xy = pieces(3)
        a = (pr_xx - ci_xy, pi_xx + cr_xy)
        b = (-ci_xy - pr_yy, cr_xy - pi_yy)
        normal = (2.0 * pi_xy + cr_xx - cr_yy, -2.0 * pr_xy + ci_xx - ci_yy)
        for q, pair in enumerate((a, b, normal)):
            block = jnp.concatenate(pair, axis=0).T
            turned[q, pl.ds(t, WIDTH, stride=4), :] = block
        return carry

    lax.fori_loop(0, TIMES, one_time, 0, unroll=4)


def build_onehot(wave_ref, onehot):
    lane = lax.broadcasted_iota(jnp.int32, (WIDTH, WIDTH), 1).astype(F32)

    def one_block(j, carry):
        column = column_of(wave_ref[pl.ds(j, 1), :].astype(F32))
        rows = pl.ds(pl.multiple_of(j * WIDTH, WIDTH), WIDTH)
        for tile in range(K // WIDTH):
            onehot[rows, tile * WIDTH : (tile + 1) * WIDTH] = jnp.where(
                column == lane + float(tile * WIDTH), 1.0, 0.0
            ).astype(BF16)
        return carry

    lax.fori_loop(0, K // WIDTH, one_block, 0)


def candidate_tables(owner_ref, block_ref, goal, named):
    owner = owner_ref[...]
    owned = jnp.where(
        lax.broadcasted_iota(jnp.int32, (BANDS, CANDS), 0) == owner, 1.0, 0.0
    )
    order = jnp.where(
        lax.broadcasted_iota(jnp.int32, (CANDS, CANDS), 0)
        < lax.broadcasted_iota(jnp.int32, (CANDS, CANDS), 1),
        1.0,
        0.0,
    ).astype(BF16)
    earlier = jnp.dot(owned.astype(BF16), order, preferred_element_type=F32)
    slot = jnp.sum(earlier * owned, axis=0, keepdims=True).astype(jnp.int32)
    target = (slot & 3) * WIDTH + owner * 4 + (slot >> 2)
    goal[...] = jnp.where(
        lax.broadcasted_iota(jnp.int32, (4 * WIDTH, CANDS), 0) == target, 1.0, 0.0
    ).astype(BF16)
    cells = jnp.where(
        lax.broadcasted_iota(jnp.int32, (256, CANDS), 0) == block_ref[...], 1.0, 0.0
    )
    named[...] = cells.T.astype(BF16)


def join_plane(plane, coeffs, ordered_in):
    pick = lax.broadcasted_iota(jnp.int32, (48, WIDTH), 1) < 64
    for j in range(PLANE // 2):
        a = coeffs[plane * PLANE + 2 * j].astype(F32)
        b = coeffs[plane * PLANE + 2 * j + 1].astype(F32)
        real = jnp.where(pick, a, pltpu.roll(b, 64, 1))
        imag = jnp.where(pick, pltpu.roll(a, 64, 1), b)
        ordered_in[0:48, j * WIDTH : (j + 1) * WIDTH] = real.astype(BF16)
        ordered_in[48:96, j * WIDTH : (j + 1) * WIDTH] = imag.astype(BF16)


def order_plane(plane, number, ordered_in, onehot, ordered, spread):
    pick = lax.broadcasted_iota(jnp.int32, (8, WIDTH), 1) < 64
    depth = PLANE * SLOTS
    rows = pl.ds(pl.multiple_of(plane * depth, depth), depth)
    for j in range(8):
        at = slice(256 * j, 256 * (j + 1))
        part = jnp.dot(ordered_in[...], onehot[rows, at], preferred_element_type=F32)
        if number > 0:
            part = part + ordered[:, at]
        if number < PLANES - 1:
            ordered[:, at] = part
            continue
        for tile in range(2):
            h = 4 * j + 2 * tile
            for c in range(2):
                for f in range(3):
                    at = c * 48 + f * 16
                    a = part[at : at + 8, tile * WIDTH : (tile + 1) * WIDTH]
                    b = part[at + 8 : at + 16, tile * WIDTH : (tile + 1) * WIDTH]
                    to = c * 24 + f * 8
                    spread[h * 48 + to : h * 48 + to + 8, :] = jnp.where(
                        pick, a, pltpu.roll(b, 64, 1)
                    )
                    spread[(h + 1) * 48 + to : (h + 1) * 48 + to + 8, :] = jnp.where(
                        pick, pltpu.roll(a, 64, 1), b
                    )


def synthesis(band, spread, tables, vort_out, okubo_out, table):
    first_ref, twiddle_ref, second_ref, fit_ref, fit_rows = tables
    southern = band >= BANDS // 2
    for t in range(TIMES):
        for rr in range(2):
            row_low = jnp.where(southern, 3 - rr, rr)
            row_high = jnp.where(southern, 1 - rr, 2 + rr)
            parts = []
            for f in range(3):
                i = f * 8 + rr * 4 + t
                c = jnp.concatenate(
                    [spread[pl.ds(i, 32, stride=48), :], spread[pl.ds(24 + i, 32, stride=48), :]],
                    axis=0,
                ).T.astype(BF16)
                z = jnp.dot(
                    jnp.concatenate([c, c], axis=1), first_ref[...], preferred_element_type=F32
                )
                zr, zi = z[:, :WIDTH], z[:, WIDTH:]
                tc, ts = twiddle_ref[0], twiddle_ref[1]
                parts.append(jnp.concatenate([zr * tc - zi * ts, zr * ts + zi * tc], axis=0))
            z = jnp.concatenate(parts, axis=1)
            high = z.astype(BF16)
            low = (z - high.astype(F32)).astype(BF16)
            grid = jnp.dot(
                second_ref[...],
                jnp.concatenate([high, high, low], axis=0),
                preferred_element_type=F32,
            )
            a = grid[:, :WIDTH]
            b = grid[:, WIDTH : 2 * WIDTH]
            normal = grid[:, 2 * WIDTH :]
            vort = a - b
            okubo = normal * normal + 4.0 * (a * b)
            vort_out[t, pl.ds(row_low, 64, stride=4), :] = vort[:64]
            vort_out[t, pl.ds(row_high, 64, stride=4), :] = vort[64:]
            okubo_out[t, pl.ds(row_low, 64, stride=4), :] = okubo[:64]
            okubo_out[t, pl.ds(row_high, 64, stride=4), :] = okubo[64:]
            both = jnp.concatenate([vort, okubo], axis=1)
            high = both.astype(BF16)
            low = (both - high.astype(F32)).astype(BF16)
            from_high = jnp.dot(high, fit_ref[...], preferred_element_type=F32)
            from_low = jnp.dot(low, fit_ref[...], preferred_element_type=F32)
            fits = from_high + pltpu.roll(from_high, WIDTH - 32, 1) + from_low
            fits = (
                fits[:64] * fit_rows[pl.ds(row_low, 1), :]
                + fits[64:] * fit_rows[pl.ds(row_high, 1), :]
            )
            if rr == 0:
                table[t * 64 : (t + 1) * 64, :] = fits
            else:
                table[t * 64 : (t + 1) * 64, :] += fits


def pick_candidates(goal, named, table):
    values = table[...]
    high = values.astype(BF16).astype(F32)
    low = values - high
    chosen = jnp.dot(
        named[...],
        jnp.concatenate([high, low], axis=1).astype(BF16),
        preferred_element_type=F32,
    )
    total = jnp.zeros((WIDTH, 2 * WIDTH), F32)
    for g in range(4):
        high = chosen[:, :WIDTH]
        low = chosen[:, WIDTH:]
        if g:
            high = pltpu.roll(high, 32 * g, 1)
            low = pltpu.roll(low, 32 * g, 1)
        total += jnp.dot(
            goal[g * WIDTH : (g + 1) * WIDTH, :],
            jnp.concatenate([high, low], axis=1).astype(BF16),
            preferred_element_type=F32,
        )
    return total[:, :WIDTH] + total[:, WIDTH:]


def whole_kernel(
    spec_hbm,
    leg_hbm,
    wave_ref,
    owner_ref,
    block_ref,
    degree_ref,
    rows_ref,
    first_ref,
    twiddle_ref,
    second_ref,
    fit_ref,
    fit_rows,
    vort_hbm,
    okubo_hbm,
    fits_out,
    spec,
    leg,
    scaled,
    factor,
    columns,
    sums,
    turned,
    send,
    recv,
    onehot,
    goal,
    named,
    ordered_in,
    ordered,
    spread,
    vort,
    okubo,
    table,
    outgoing,
    arrived,
    lines,
    spec_sem,
    leg_sem,
    out_sem,
    send_sem,
    recv_sem,
    send_fit,
    recv_fit,
):
    lev = lax.axis_index("lev")
    me = lax.axis_index("band")
    rank = lev * BANDS + me

    def spec_copy(g):
        window = pl.ds(pl.multiple_of(g * GROUP, GROUP), GROUP)
        return pltpu.make_async_copy(
            spec_hbm.at[:, window, :], spec.at[:, window, :], spec_sem.at[g]
        )

    def leg_copy(g):
        window = pl.ds(g * LEG_PART, LEG_PART)
        return pltpu.make_async_copy(leg_hbm.at[window], leg.at[window], leg_sem.at[g])

    for g in range(SLOTS // GROUP):
        spec_copy(g).start()
        for part in range(GROUP // LEG_PART):
            leg_copy(g * (GROUP // LEG_PART) + part).start()

    barrier = pltpu.get_barrier_semaphore()
    greet_all(barrier, rank)

    columns[...] = column_of(wave_ref[pl.ds(me // 2, 1), :].astype(F32))
    first = pl.multiple_of(lax.rem(me, 2) * SLOTS, SLOTS)
    waits = (lambda g: spec_copy(g).wait(), lambda g: leg_copy(g).wait())
    legendre_sums(first, waits, spec, leg, degree_ref, columns, scaled, factor, sums)
    combine_rows(first, columns, rows_ref, sums, turned)

    pl.semaphore_wait(barrier, MEMBERS - 1)

    my_plane = me // PLANE
    my_place = lax.rem(me, PLANE)

    def fill(d):
        p = jnp.where(d < BANDS // 2, d, BANDS + BANDS // 2 - 1 - d)
        for q in range(3):
            send[d, 16 * q : 16 * q + 16, :] = turned[
                q, pl.ds(pl.multiple_of(p * 16, 16), 16), :
            ].astype(BF16)

    def message(d):
        return pltpu.make_async_remote_copy(
            src_ref=send.at[d],
            dst_ref=recv.at[me],
            send_sem=send_sem.at[d],
            recv_sem=recv_sem.at[me],
            device_id={"band": d},
            device_id_type=MESH,
        )

    def arrival(source):
        return pltpu.make_async_remote_copy(
            src_ref=send.at[source],
            dst_ref=recv.at[source],
            send_sem=send_sem.at[source],
            recv_sem=recv_sem.at[source],
            device_id={"band": source},
            device_id_type=MESH,
        )

    shifts = (0, 1, 3, 2)
    for shift in shifts:
        plane = lax.rem(my_plane + shift, PLANES)

        def post(k, carry, plane=plane):
            d = plane * PLANE + lax.rem(my_place + k, PLANE)
            fill(d)
            message(d).start()
            return carry

        lax.fori_loop(0 if shift else 1, PLANE, post, 0)
    fill(me)
    recv[me] = send[me]

    build_onehot(wave_ref, onehot)
    candidate_tables(owner_ref, block_ref, goal, named)

    for number, shift in enumerate(shifts):
        plane = lax.rem(my_plane + PLANES - shift, PLANES)

        def take(k, carry, plane=plane):
            arrival(plane * PLANE + lax.rem(my_place + k, PLANE)).wait_recv()
            return carry

        lax.fori_loop(0 if shift else 1, PLANE, take, 0)
        join_plane(plane, recv, ordered_in)
        order_plane(plane, number, ordered_in, onehot, ordered, spread)

    tables = (first_ref, twiddle_ref, second_ref, fit_ref, fit_rows)
    synthesis(me, spread, tables, vort, okubo, table)
    vort_copy = pltpu.make_async_copy(vort, vort_hbm, out_sem.at[0])
    okubo_copy = pltpu.make_async_copy(okubo, okubo_hbm, out_sem.at[1])
    vort_copy.start()
    okubo_copy.start()

    outgoing[...] = pick_candidates(goal, named, table).reshape(BANDS, 4, WIDTH)

    def fit_copy(other, place):
        return pltpu.make_async_remote_copy(
            src_ref=outgoing.at[lax.rem(other, BANDS)],
            dst_ref=arrived.at[place],
            send_sem=send_fit.at[other],
            recv_sem=recv_fit.at[place],
            device_id={"lev": other // BANDS, "band": lax.rem(other, BANDS)},
            device_id_type=MESH,
        )

    def post_fit(k, carry):
        fit_copy(lax.rem(rank + k, MEMBERS), rank).start()
        return carry

    lax.fori_loop(1, MEMBERS, post_fit, 0)
    arrived[rank] = outgoing[me]

    def take_fit(k, carry):
        other = lax.rem(rank + k, MEMBERS)
        fit_copy(other, other).wait_recv()
        return carry

    lax.fori_loop(1, MEMBERS, take_fit, 0)

    for r in range(ROUNDS):
        line = (arrived[0:32, r, :] + arrived[32:64, r, :]) + (
            arrived[64:96, r, :] + arrived[96:128, r, :]
        )
        for g in range(4):
            value = pltpu.roll(line, WIDTH - 32 * g, 1) if g else line
            lines[pl.ds(4 * r + g, BANDS, stride=CAP), :] = value
    fits_out[...] = lines[...].T[:20, :]

    def sent(d, carry):
        @pl.when(d != me)
        def _():
            message(d).wait_send()

        return carry

    lax.fori_loop(0, BANDS, sent, 0)

    def sent_fit(k, carry):
        fit_copy(lax.rem(rank + k, MEMBERS), rank).wait_send()
        return carry

    lax.fori_loop(1, MEMBERS, sent_fit, 0)
    vort_copy.wait()
    okubo_copy.wait()


def whole(spectra, legendre, waves, owner, block):
    vmem = pl.BlockSpec(memory_space=pltpu.VMEM)
    hbm = pl.BlockSpec(memory_space=pl.ANY)
    fit_table, fit_rows = fit_tables()
    grid = jax.ShapeDtypeStruct((TIMES, 256, WIDTH), F32)
    return pl.pallas_call(
        whole_kernel,
        out_shape=(grid, grid, jax.ShapeDtypeStruct((20, BANDS * CAP), F32)),
        in_specs=[hbm, hbm] + [vmem] * 10,
        out_specs=(hbm, hbm, vmem),
        scratch_shapes=[
            pltpu.VMEM((16, SLOTS, K), BF16),
            pltpu.VMEM((SLOTS, HALF, K), BF16),
            pltpu.VMEM((K // WIDTH, 16 * GROUP, WIDTH), F32),
            pltpu.VMEM((GROUP, K), F32),
            pltpu.VMEM((WIDTH, WIDTH), F32),
            pltpu.VMEM((SLOTS * 16, WIDTH), F32),
            pltpu.VMEM((3, 4 * WIDTH, WIDTH), F32),
            pltpu.VMEM((BANDS, 48, WIDTH), BF16),
            pltpu.VMEM((BANDS, 48, WIDTH), BF16),
            pltpu.VMEM((K, K), BF16),
            pltpu.VMEM((4 * WIDTH, CANDS), BF16),
            pltpu.VMEM((CANDS, 256), BF16),
            pltpu.VMEM((96, PLANE * SLOTS), BF16),
            pltpu.VMEM((96, K), F32),
            pltpu.VMEM((32 * 48, WIDTH), F32),
            pltpu.VMEM((TIMES, 256, WIDTH), F32),
            pltpu.VMEM((TIMES, 256, WIDTH), F32),
            pltpu.VMEM((256, WIDTH), F32),
            pltpu.VMEM((BANDS, 4, WIDTH), F32),
            pltpu.VMEM((MEMBERS, 4, WIDTH), F32),
            pltpu.VMEM((BANDS * CAP, WIDTH), F32),
            pltpu.SemaphoreType.DMA((SLOTS // GROUP,)),
            pltpu.SemaphoreType.DMA((SLOTS // LEG_PART,)),
            pltpu.SemaphoreType.DMA((2,)),
            pltpu.SemaphoreType.DMA((BANDS,)),
            pltpu.SemaphoreType.DMA((BANDS,)),
            pltpu.SemaphoreType.DMA((MEMBERS,)),
            pltpu.SemaphoreType.DMA((MEMBERS,)),
        ],
        compiler_params=pltpu.CompilerParams(
            collective_id=0, has_side_effects=True, vmem_limit_bytes=56 * 1024 * 1024
        ),
        name="spectral_analysis",
    )(
        spectra,
        legendre,
        waves,
        owner,
        block,
        degree_table(),
        row_table(),
        first_table(),
        twiddle_table(),
        second_table(),
        fit_table,
        fit_rows,
    )


def local(spectra, legendre, wave_order, cand_block, cand_owner):
    vort, okubo, fits = whole(
        spectra.reshape(16, SLOTS, K),
        legendre,
        wave_order.reshape(K // WIDTH, WIDTH),
        cand_owner.reshape(1, CANDS),
        cand_block.reshape(1, CANDS),
    )

    def rows(field):
        shaped = field.reshape(TIMES, 64, 4, WIDTH).transpose(0, 2, 1, 3)
        return shaped.reshape(1, TIMES, 4, NLON)

    return rows(vort), rows(okubo), fits.T


def solution(mesh):
    placed = (
        P("lev", None, None, None, "band", None),
        P("band", None, None),
        P(),
        P("band"),
        P("band", None),
    )
    return jax.shard_map(
        local,
        mesh=mesh,
        in_specs=placed,
        out_specs=(P("lev", None, "band", None), P("lev", None, "band", None), P("band", None)),
        check_vma=False,
    )
```

time: 68 us -> 50 us (0.74)
  Pallas kernels: 64.4 us -> 43.9 us
  local copies, waits for them, and re-layouts: 2.65 us -> 5.12 us
    pallas_call x3 -> x1, Pallas kernels: 64.4 us -> 43.9 us  [whole(): pl.pallas_call(whole_kernel, out_shape=(grid, grid, jax.ShapeDtypeStruct(...]
    unnamed x18 -> x3, local copies, waits for them, and re-layouts: 2.65 us -> 5.12 us
where the time goes in v2:
time: 50 us; the launch traced here: 49.7 us
  Pallas kernels  43.9 us (88%)
  local copies, waits for them, and re-layouts  5.12 us (10%)
  between operations  0.64 us (1%)
    pallas_call x1, Pallas kernels, whole(): pl.pallas_call(whole_kernel, out_shape=(grid, grid, jax.ShapeDtypeStruct(...  43.9 us
    unnamed x3, local copies, waits for them, and re-layouts  5.12 us

profile of v2, /device:TPU:1, one launch (start us, length us, event | category | flops | bytes accessed | tf_op | source)
XLA Modules:
  0.0 49.7 jit_solution(9694340928718094705)
XLA Ops:
  0.6 43.9 %spectral_analysis.1 = (f32[4,256,128]{2,1,0:T(8,128)}, f32[4,256,128]{2,1,0:T(8,128)}, f32[20,384]{1,0:T(8,128)}) custom-call(bf16[16,64,2048]{2,1,0:T(8,128)(2,1)} %bitcast.15, bf16[64,64,2048]{2,1,0:T(8,128)(2,1)} %leg_hbm.1, s32[16,128]{1,0:T(8,128)} %bitcast.19, s32[1,192]{1,0:T(1,128)} %bitcast.20, s32[1,192]{1,0:T(1,128)} %bitcast.21, ...), custom_call_target="tpu_custom_call" | custom-call | tf_op jit(solution)/shard_map/spectral_analysis/pallas_call | solution.py:601
  44.5 1.9 %copy.20 = f32[1,4,4,8192]{3,2,1,0:T(4,128)} copy(f32[1,4,4,8192]{3,2,1,0:T(4,128)} %bitcast.17) | data formatting | bytes 1048576
  46.4 1.9 %copy.21 = f32[1,4,4,8192]{3,2,1,0:T(4,128)} copy(f32[1,4,4,8192]{3,2,1,0:T(4,128)} %bitcast.16) | data formatting | bytes 1048576
  48.3 1.4 %copy.22 = f32[384,20]{0,1:T(8,128)} copy(f32[384,20]{0,1:T(8,128)} %bitcast.18) | data formatting | bytes 61440

commit v3 on v2

--- a/solution.py
+++ b/solution.py
@@ -135,18 +135,27 @@
     return jnp.broadcast_to(row, (WIDTH, WIDTH)).T
 
 
-def greet_all(barrier, rank):
+def greet_peers(semaphore, lev, me):
+    for k in range(1, LEVS):
+        pl.semaphore_signal(
+            semaphore,
+            inc=1,
+            device_id={"lev": lax.rem(lev + k, LEVS), "band": me},
+            device_id_type=MESH,
+        )
+
+
+def greet_band(semaphore, lev, me):
     def greet(k, carry):
-        other = lax.rem(rank + k, MEMBERS)
         pl.semaphore_signal(
-            barrier,
+            semaphore,
             inc=1,
-            device_id={"lev": other // BANDS, "band": lax.rem(other, BANDS)},
+            device_id={"lev": lev, "band": lax.rem(me + k, BANDS)},
             device_id_type=MESH,
         )
         return carry
 
-    lax.fori_loop(1, MEMBERS, greet, 0)
+    lax.fori_loop(1, BANDS, greet, 0)
 
 
 def legendre_sums(first, waits, spec, leg, degree_ref, columns, scaled, factor, sums):
@@ -413,8 +422,8 @@
     second_ref,
     fit_ref,
     fit_rows,
-    vort_hbm,
-    okubo_hbm,
+    vort_out,
+    okubo_out,
     fits_out,
     spec,
     leg,
@@ -431,19 +440,17 @@
     ordered_in,
     ordered,
     spread,
-    vort,
-    okubo,
     table,
     outgoing,
     arrived,
     lines,
     spec_sem,
     leg_sem,
-    out_sem,
     send_sem,
     recv_sem,
     send_fit,
     recv_fit,
+    level_sem,
 ):
     lev = lax.axis_index("lev")
     me = lax.axis_index("band")
@@ -465,7 +472,8 @@
             leg_copy(g * (GROUP // LEG_PART) + part).start()
 
     barrier = pltpu.get_barrier_semaphore()
-    greet_all(barrier, rank)
+    greet_peers(barrier, lev, me)
+    greet_band(barrier, lev, me)
 
     columns[...] = column_of(wave_ref[pl.ds(me // 2, 1), :].astype(F32))
     first = pl.multiple_of(lax.rem(me, 2) * SLOTS, SLOTS)
@@ -473,98 +481,83 @@
     legendre_sums(first, waits, spec, leg, degree_ref, columns, scaled, factor, sums)
     combine_rows(first, columns, rows_ref, sums, turned)
 
-    pl.semaphore_wait(barrier, MEMBERS - 1)
+    for p in range(BANDS):
+        for q in range(3):
+            send[p, 16 * q : 16 * q + 16, :] = turned[q, p * 16 : p * 16 + 16, :].astype(BF16)
+
+    pl.semaphore_wait(barrier, BANDS - 1 + LEVS - 1)
 
     my_plane = me // PLANE
     my_place = lax.rem(me, PLANE)
 
-    def fill(d):
-        p = jnp.where(d < BANDS // 2, d, BANDS + BANDS // 2 - 1 - d)
-        for q in range(3):
-            send[d, 16 * q : 16 * q + 16, :] = turned[
-                q, pl.ds(pl.multiple_of(p * 16, 16), 16), :
-            ].astype(BF16)
-
-    def message(d):
+    def place(d):
+        return jnp.where(d < BANDS // 2, d, BANDS + BANDS // 2 - 1 - d)
+
+    shifts = (0, 1, 3, 2)
+    for number, shift in enumerate(shifts):
+        plane = lax.rem(my_plane + shift, PLANES)
+        for k in range(0 if shift else 1, PLANE):
+            d = plane * PLANE + lax.rem(my_place + k, PLANE)
+            pltpu.make_async_remote_copy(
+                src_ref=send.at[place(d)],
+                dst_ref=recv.at[me],
+                send_sem=send_sem,
+                recv_sem=recv_sem.at[number],
+                device_id={"lev": lev, "band": d},
+                device_id_type=MESH,
+            ).start()
+    recv[me] = send[place(me)]
+    greet_peers(level_sem, lev, me)
+
+    def bulk(count, number):
         return pltpu.make_async_remote_copy(
-            src_ref=send.at[d],
-            dst_ref=recv.at[me],
-            send_sem=send_sem.at[d],
-            recv_sem=recv_sem.at[me],
-            device_id={"band": d},
+            src_ref=send.at[pl.ds(0, count)],
+            dst_ref=recv.at[pl.ds(0, count)],
+            send_sem=send_sem,
+            recv_sem=recv_sem.at[number],
+            device_id={"lev": lev, "band": me},
             device_id_type=MESH,
         )
 
-    def arrival(source):
-        return pltpu.make_async_remote_copy(
-            src_ref=send.at[source],
-            dst_ref=recv.at[source],
-            send_sem=send_sem.at[source],
-            recv_sem=recv_sem.at[source],
-            device_id={"band": source},
-            device_id_type=MESH,
-        )
-
-    shifts = (0, 1, 3, 2)
-    for shift in shifts:
-        plane = lax.rem(my_plane + shift, PLANES)
-
-        def post(k, carry, plane=plane):
-            d = plane * PLANE + lax.rem(my_place + k, PLANE)
-            fill(d)
-            message(d).start()
-            return carry
-
-        lax.fori_loop(0 if shift else 1, PLANE, post, 0)
-    fill(me)
-    recv[me] = send[me]
-
     build_onehot(wave_ref, onehot)
     candidate_tables(owner_ref, block_ref, goal, named)
 
     for number, shift in enumerate(shifts):
         plane = lax.rem(my_plane + PLANES - shift, PLANES)
-
-        def take(k, carry, plane=plane):
-            arrival(plane * PLANE + lax.rem(my_place + k, PLANE)).wait_recv()
-            return carry
-
-        lax.fori_loop(0 if shift else 1, PLANE, take, 0)
+        bulk(PLANE if shift else PLANE - 1, number).wait_recv()
         join_plane(plane, recv, ordered_in)
         order_plane(plane, number, ordered_in, onehot, ordered, spread)
 
     tables = (first_ref, twiddle_ref, second_ref, fit_ref, fit_rows)
-    synthesis(me, spread, tables, vort, okubo, table)
-    vort_copy = pltpu.make_async_copy(vort, vort_hbm, out_sem.at[0])
-    okubo_copy = pltpu.make_async_copy(okubo, okubo_hbm, out_sem.at[1])
-    vort_copy.start()
-    okubo_copy.start()
-
+    synthesis(me, spread, tables, vort_out, okubo_out, table)
     outgoing[...] = pick_candidates(goal, named, table).reshape(BANDS, 4, WIDTH)
 
-    def fit_copy(other, place):
-        return pltpu.make_async_remote_copy(
-            src_ref=outgoing.at[lax.rem(other, BANDS)],
-            dst_ref=arrived.at[place],
-            send_sem=send_fit.at[other],
-            recv_sem=recv_fit.at[place],
-            device_id={"lev": other // BANDS, "band": lax.rem(other, BANDS)},
+    pl.semaphore_wait(level_sem, LEVS - 1)
+
+    def post_fit(k, carry):
+        other = lax.rem(rank + k, MEMBERS)
+        owner = lax.rem(other, BANDS)
+        pltpu.make_async_remote_copy(
+            src_ref=outgoing.at[owner],
+            dst_ref=arrived.at[rank],
+            send_sem=send_fit,
+            recv_sem=recv_fit,
+            device_id={"lev": other // BANDS, "band": owner},
             device_id_type=MESH,
-        )
-
-    def post_fit(k, carry):
-        fit_copy(lax.rem(rank + k, MEMBERS), rank).start()
+        ).start()
         return carry
 
     lax.fori_loop(1, MEMBERS, post_fit, 0)
     arrived[rank] = outgoing[me]
-
-    def take_fit(k, carry):
-        other = lax.rem(rank + k, MEMBERS)
-        fit_copy(other, other).wait_recv()
-        return carry
-
-    lax.fori_loop(1, MEMBERS, take_fit, 0)
+    everything = pltpu.make_async_remote_copy(
+        src_ref=arrived.at[pl.ds(0, MEMBERS - 1)],
+        dst_ref=arrived.at[pl.ds(0, MEMBERS - 1)],
+        send_sem=send_fit,
+        recv_sem=recv_fit,
+        device_id={"lev": lev, "band": me},
+        device_id_type=MESH,
+    )
+    everything.wait_recv()
 
     for r in range(ROUNDS):
         line = (arrived[0:32, r, :] + arrived[32:64, r, :]) + (
@@ -575,22 +568,46 @@
             lines[pl.ds(4 * r + g, BANDS, stride=CAP), :] = value
     fits_out[...] = lines[...].T[:20, :]
 
-    def sent(d, carry):
-        @pl.when(d != me)
-        def _():
-            message(d).wait_send()
-
-        return carry
-
-    lax.fori_loop(0, BANDS, sent, 0)
-
-    def sent_fit(k, carry):
-        fit_copy(lax.rem(rank + k, MEMBERS), rank).wait_send()
-        return carry
-
-    lax.fori_loop(1, MEMBERS, sent_fit, 0)
-    vort_copy.wait()
-    okubo_copy.wait()
+    bulk(BANDS - 1, 0).wait_send()
+    everything.wait_send()
+
+
+def copy_kernel(*refs):
+    sources, targets, held, come, go = refs[:3], refs[3:6], refs[6:9], refs[9], refs[10]
+    pieces = [(i, t) for i in range(2) for t in range(TIMES)] + [(2, None)]
+
+    def view(ref, t):
+        return ref if t is None else ref.at[t]
+
+    inward = [
+        pltpu.make_async_copy(view(sources[i], t), view(held[i], t), come.at[n])
+        for n, (i, t) in enumerate(pieces)
+    ]
+    outward = [
+        pltpu.make_async_copy(view(held[i], t), view(targets[i], t), go.at[n])
+        for n, (i, t) in enumerate(pieces)
+    ]
+    for copy in inward:
+        copy.start()
+    for n in range(len(pieces)):
+        inward[n].wait()
+        outward[n].start()
+    for copy in outward:
+        copy.wait()
+
+
+def copied(*results):
+    hbm = pl.BlockSpec(memory_space=pl.ANY)
+    return pl.pallas_call(
+        copy_kernel,
+        out_shape=tuple(jax.ShapeDtypeStruct(r.shape, r.dtype) for r in results),
+        in_specs=[hbm] * 3,
+        out_specs=(hbm,) * 3,
+        scratch_shapes=[pltpu.VMEM(r.shape, r.dtype) for r in results]
+        + [pltpu.SemaphoreType.DMA((2 * TIMES + 1,)), pltpu.SemaphoreType.DMA((2 * TIMES + 1,))],
+        compiler_params=pltpu.CompilerParams(vmem_limit_bytes=60 * 1024 * 1024),
+        name="results",
+    )(*results)
 
 
 def whole(spectra, legendre, waves, owner, block):
@@ -602,7 +619,7 @@
         whole_kernel,
         out_shape=(grid, grid, jax.ShapeDtypeStruct((20, BANDS * CAP), F32)),
         in_specs=[hbm, hbm] + [vmem] * 10,
-        out_specs=(hbm, hbm, vmem),
+        out_specs=(vmem, vmem, vmem),
         scratch_shapes=[
             pltpu.VMEM((16, SLOTS, K), BF16),
             pltpu.VMEM((SLOTS, HALF, K), BF16),
@@ -619,19 +636,17 @@
             pltpu.VMEM((96, PLANE * SLOTS), BF16),
             pltpu.VMEM((96, K), F32),
             pltpu.VMEM((32 * 48, WIDTH), F32),
-            pltpu.VMEM((TIMES, 256, WIDTH), F32),
-            pltpu.VMEM((TIMES, 256, WIDTH), F32),
             pltpu.VMEM((256, WIDTH), F32),
             pltpu.VMEM((BANDS, 4, WIDTH), F32),
             pltpu.VMEM((MEMBERS, 4, WIDTH), F32),
             pltpu.VMEM((BANDS * CAP, WIDTH), F32),
             pltpu.SemaphoreType.DMA((SLOTS // GROUP,)),
             pltpu.SemaphoreType.DMA((SLOTS // LEG_PART,)),
-            pltpu.SemaphoreType.DMA((2,)),
-            pltpu.SemaphoreType.DMA((BANDS,)),
-            pltpu.SemaphoreType.DMA((BANDS,)),
-            pltpu.SemaphoreType.DMA((MEMBERS,)),
-            pltpu.SemaphoreType.DMA((MEMBERS,)),
+            pltpu.SemaphoreType.DMA,
+            pltpu.SemaphoreType.DMA((PLANES,)),
+            pltpu.SemaphoreType.DMA,
+            pltpu.SemaphoreType.DMA,
+            pltpu.SemaphoreType.REGULAR,
         ],
         compiler_params=pltpu.CompilerParams(
             collective_id=0, has_side_effects=True, vmem_limit_bytes=56 * 1024 * 1024
@@ -654,13 +669,14 @@
 
 
 def local(spectra, legendre, wave_order, cand_block, cand_owner):
-    vort, okubo, fits = whole(
+    results = whole(
         spectra.reshape(16, SLOTS, K),
         legendre,
         wave_order.reshape(K // WIDTH, WIDTH),
         cand_owner.reshape(1, CANDS),
         cand_block.reshape(1, CANDS),
     )
+    vort, okubo, fits = copied(*results)
 
     def rows(field):
         shaped = field.reshape(TIMES, 64, 4, WIDTH).transpose(0, 2, 1, 3)

time: 50 us -> 42.7 us (0.85)
  local copies, waits for them, and re-layouts: 5.12 us -> 0 us
  Pallas kernels: 43.9 us -> 41.9 us
    unnamed x3 -> x0, local copies, waits for them, and re-layouts: 5.12 us -> none
    pallas_call x1, Pallas kernels: 43.9 us -> 39.8 us  [whole(): pl.pallas_call(whole_kernel, out_shape=(grid, grid, jax.ShapeDtypeStruct(...]
    pallas_call x0 -> x1, Pallas kernels: none -> 2.11 us  [copied(): pl.pallas_call(copy_kernel, out_shape=tuple((jax.ShapeDtypeStruct(r.shape...]
where the time goes in v3:
time: 42.7 us; the launch traced here: 42.5 us
  Pallas kernels  41.9 us (98%)
  between operations  0.64 us (1%)
    pallas_call x1, Pallas kernels, whole(): pl.pallas_call(whole_kernel, out_shape=(grid, grid, jax.ShapeDtypeStruct(...  39.8 us
    pallas_call x1, Pallas kernels, copied(): pl.pallas_call(copy_kernel, out_shape=tuple((jax.ShapeDtypeStruct(r.shape...  2.11 us

profile of v3, /device:TPU:1, one launch (start us, length us, event | category | flops | bytes accessed | tf_op | source)
XLA Modules:
  0.0 42.5 jit_solution(18311466205354207591)
XLA Ops:
  0.6 39.8 %spectral_analysis.1 = (f32[4,256,128]{2,1,0:T(8,128)}, f32[4,256,128]{2,1,0:T(8,128)}, f32[20,384]{1,0:T(8,128)}) custom-call(bf16[16,64,2048]{2,1,0:T(8,128)(2,1)} %bitcast.15, bf16[64,64,2048]{2,1,0:T(8,128)(2,1)} %leg_hbm.1, s32[16,128]{1,0:T(8,128)} %bitcast.16, s32[1,192]{1,0:T(1,128)} %bitcast.17, s32[1,192]{1,0:T(1,128)} %bitcast.18, ...), custom_call_target="tpu_custom_call" | custom-call | tf_op jit(solution)/shard_map/spectral_analysis/pallas_call | solution.py:618
  40.4 2.1 %results.1 = (f32[4,256,128]{2,1,0:T(8,128)}, f32[4,256,128]{2,1,0:T(8,128)}, f32[20,384]{1,0:T(8,128)}) custom-call(f32[4,256,128]{2,1,0:T(8,128)} %get-tuple-element.9.refs_0_, f32[4,256,128]{2,1,0:T(8,128)} %get-tuple-element.10.refs_1_, f32[20,384]{1,0:T(8,128)} %get-tuple-element.11.refs_2_), custom_call_target="tpu_custom_call" | custom-call | tf_op jit(solution)/shard_map/results/pallas_call | solution.py:601

commit v4 on v3

--- a/solution.py
+++ b/solution.py
@@ -27,7 +27,8 @@
 WIDTH = 128
 CANDS = 192
 CAP = 12
-ROUNDS = CAP // 4
+PACK = 6
+VALUES = 20
 
 
 def bf16_split(table):
@@ -176,7 +177,7 @@
                 scaled[tile, window, :] = part[:, tile * WIDTH : (tile + 1) * WIDTH]
             return inner
 
-        lax.fori_loop(0, 16, scale, 0)
+        lax.fori_loop(0, 16, scale, 0, unroll=4)
 
         def one_slot(i, inner):
             even = jnp.concatenate(
@@ -197,17 +198,11 @@
             )
             return inner
 
-        for part in range(GROUP // LEG_PART):
-            leg_wait(g * (GROUP // LEG_PART) + part)
-            lax.fori_loop(
-                part * LEG_PART, (part + 1) * LEG_PART, one_slot, 0, unroll=LEG_PART
-            )
+        leg_wait(g)
+        lax.fori_loop(0, GROUP, one_slot, 0, unroll=GROUP)
         return carry
 
     lax.fori_loop(0, SLOTS // GROUP, one_group, 0)
-
-
-LEG_PART = 8
 
 
 def combine_rows(first, columns, rows_ref, sums, turned):
@@ -283,9 +278,10 @@
     ).astype(BF16)
     earlier = jnp.dot(owned.astype(BF16), order, preferred_element_type=F32)
     slot = jnp.sum(earlier * owned, axis=0, keepdims=True).astype(jnp.int32)
-    target = (slot & 3) * WIDTH + owner * 4 + (slot >> 2)
+    second = jnp.where(slot >= PACK, 1, 0)
+    target = (slot - PACK * second) * (2 * BANDS) + owner * 2 + second
     goal[...] = jnp.where(
-        lax.broadcasted_iota(jnp.int32, (4 * WIDTH, CANDS), 0) == target, 1.0, 0.0
+        lax.broadcasted_iota(jnp.int32, (PACK * 2 * BANDS, CANDS), 0) == target, 1.0, 0.0
     ).astype(BF16)
     cells = jnp.where(
         lax.broadcasted_iota(jnp.int32, (256, CANDS), 0) == block_ref[...], 1.0, 0.0
@@ -394,15 +390,15 @@
         jnp.concatenate([high, low], axis=1).astype(BF16),
         preferred_element_type=F32,
     )
-    total = jnp.zeros((WIDTH, 2 * WIDTH), F32)
-    for g in range(4):
+    total = jnp.zeros((2 * BANDS, 2 * WIDTH), F32)
+    for g in range(PACK):
         high = chosen[:, :WIDTH]
         low = chosen[:, WIDTH:]
         if g:
-            high = pltpu.roll(high, 32 * g, 1)
-            low = pltpu.roll(low, 32 * g, 1)
+            high = pltpu.roll(high, VALUES * g, 1)
+            low = pltpu.roll(low, VALUES * g, 1)
         total += jnp.dot(
-            goal[g * WIDTH : (g + 1) * WIDTH, :],
+            goal[g * 2 * BANDS : (g + 1) * 2 * BANDS, :],
             jnp.concatenate([high, low], axis=1).astype(BF16),
             preferred_element_type=F32,
         )
@@ -440,6 +436,8 @@
     ordered_in,
     ordered,
     spread,
+    vort,
+    okubo,
     table,
     outgoing,
     arrived,
@@ -451,6 +449,7 @@
     send_fit,
     recv_fit,
     level_sem,
+    out_sem,
 ):
     lev = lax.axis_index("lev")
     me = lax.axis_index("band")
@@ -463,13 +462,12 @@
         )
 
     def leg_copy(g):
-        window = pl.ds(g * LEG_PART, LEG_PART)
+        window = pl.ds(pl.multiple_of(g * GROUP, GROUP), GROUP)
         return pltpu.make_async_copy(leg_hbm.at[window], leg.at[window], leg_sem.at[g])
 
     for g in range(SLOTS // GROUP):
         spec_copy(g).start()
-        for part in range(GROUP // LEG_PART):
-            leg_copy(g * (GROUP // LEG_PART) + part).start()
+        leg_copy(g).start()
 
     barrier = pltpu.get_barrier_semaphore()
     greet_peers(barrier, lev, me)
@@ -529,8 +527,14 @@
         order_plane(plane, number, ordered_in, onehot, ordered, spread)
 
     tables = (first_ref, twiddle_ref, second_ref, fit_ref, fit_rows)
-    synthesis(me, spread, tables, vort_out, okubo_out, table)
-    outgoing[...] = pick_candidates(goal, named, table).reshape(BANDS, 4, WIDTH)
+    synthesis(me, spread, tables, vort, okubo, table)
+    grid_copies = [
+        pltpu.make_async_copy(vort, vort_out, out_sem.at[0]),
+        pltpu.make_async_copy(okubo, okubo_out, out_sem.at[1]),
+    ]
+    for copy in grid_copies:
+        copy.start()
+    outgoing[...] = pick_candidates(goal, named, table).reshape(BANDS, 2, WIDTH)
 
     pl.semaphore_wait(level_sem, LEVS - 1)
 
@@ -547,7 +551,7 @@
         ).start()
         return carry
 
-    lax.fori_loop(1, MEMBERS, post_fit, 0)
+    lax.fori_loop(1, MEMBERS, post_fit, 0, unroll=4)
     arrived[rank] = outgoing[me]
     everything = pltpu.make_async_remote_copy(
         src_ref=arrived.at[pl.ds(0, MEMBERS - 1)],
@@ -559,17 +563,19 @@
     )
     everything.wait_recv()
 
-    for r in range(ROUNDS):
+    for r in range(CAP // PACK):
         line = (arrived[0:32, r, :] + arrived[32:64, r, :]) + (
             arrived[64:96, r, :] + arrived[96:128, r, :]
         )
-        for g in range(4):
-            value = pltpu.roll(line, WIDTH - 32 * g, 1) if g else line
-            lines[pl.ds(4 * r + g, BANDS, stride=CAP), :] = value
+        for g in range(PACK):
+            value = pltpu.roll(line, WIDTH - VALUES * g, 1) if g else line
+            lines[pl.ds(PACK * r + g, BANDS, stride=CAP), :] = value
     fits_out[...] = lines[...].T[:20, :]
 
     bulk(BANDS - 1, 0).wait_send()
     everything.wait_send()
+    for copy in grid_copies:
+        copy.wait()
 
 
 def copy_kernel(*refs):
@@ -619,7 +625,7 @@
         whole_kernel,
         out_shape=(grid, grid, jax.ShapeDtypeStruct((20, BANDS * CAP), F32)),
         in_specs=[hbm, hbm] + [vmem] * 10,
-        out_specs=(vmem, vmem, vmem),
+        out_specs=(hbm, hbm, vmem),
         scratch_shapes=[
             pltpu.VMEM((16, SLOTS, K), BF16),
             pltpu.VMEM((SLOTS, HALF, K), BF16),
@@ -631,22 +637,25 @@
             pltpu.VMEM((BANDS, 48, WIDTH), BF16),
             pltpu.VMEM((BANDS, 48, WIDTH), BF16),
             pltpu.VMEM((K, K), BF16),
-            pltpu.VMEM((4 * WIDTH, CANDS), BF16),
+            pltpu.VMEM((PACK * 2 * BANDS, CANDS), BF16),
             pltpu.VMEM((CANDS, 256), BF16),
             pltpu.VMEM((96, PLANE * SLOTS), BF16),
             pltpu.VMEM((96, K), F32),
             pltpu.VMEM((32 * 48, WIDTH), F32),
+            pltpu.VMEM((TIMES, 256, WIDTH), F32),
+            pltpu.VMEM((TIMES, 256, WIDTH), F32),
             pltpu.VMEM((256, WIDTH), F32),
-            pltpu.VMEM((BANDS, 4, WIDTH), F32),
-            pltpu.VMEM((MEMBERS, 4, WIDTH), F32),
+            pltpu.VMEM((BANDS, 2, WIDTH), F32),
+            pltpu.VMEM((MEMBERS, 2, WIDTH), F32),
             pltpu.VMEM((BANDS * CAP, WIDTH), F32),
             pltpu.SemaphoreType.DMA((SLOTS // GROUP,)),
-            pltpu.SemaphoreType.DMA((SLOTS // LEG_PART,)),
+            pltpu.SemaphoreType.DMA((SLOTS // GROUP,)),
             pltpu.SemaphoreType.DMA,
             pltpu.SemaphoreType.DMA((PLANES,)),
             pltpu.SemaphoreType.DMA,
             pltpu.SemaphoreType.DMA,
             pltpu.SemaphoreType.REGULAR,
+            pltpu.SemaphoreType.DMA((2,)),
         ],
         compiler_params=pltpu.CompilerParams(
             collective_id=0, has_side_effects=True, vmem_limit_bytes=56 * 1024 * 1024

time: 42.7 us -> 39 us (0.913)
  Pallas kernels: 41.9 us -> 38.2 us
    pallas_call x1, Pallas kernels: 39.8 us -> 36.1 us  [whole(): pl.pallas_call(whole_kernel, out_shape=(grid, grid, jax.ShapeDtypeStruct(...]
where the time goes in v4:
time: 39 us; the launch traced here: 38.8 us
  Pallas kernels  38.2 us (98%)
  between operations  0.64 us (2%)
    pallas_call x1, Pallas kernels, whole(): pl.pallas_call(whole_kernel, out_shape=(grid, grid, jax.ShapeDtypeStruct(...  36.1 us
    pallas_call x1, Pallas kernels, copied(): pl.pallas_call(copy_kernel, out_shape=tuple((jax.ShapeDtypeStruct(r.shape...  2.11 us

profile of v4, /device:TPU:1, one launch (start us, length us, event | category | flops | bytes accessed | tf_op | source)
XLA Modules:
  0.0 38.8 jit_solution(13176923920030156856)
XLA Ops:
  0.6 36.1 %spectral_analysis.1 = (f32[4,256,128]{2,1,0:T(8,128)}, f32[4,256,128]{2,1,0:T(8,128)}, f32[20,384]{1,0:T(8,128)}) custom-call(bf16[16,64,2048]{2,1,0:T(8,128)(2,1)} %bitcast.15, bf16[64,64,2048]{2,1,0:T(8,128)(2,1)} %leg_hbm.1, s32[16,128]{1,0:T(8,128)} %bitcast.16, s32[1,192]{1,0:T(1,128)} %bitcast.17, s32[1,192]{1,0:T(1,128)} %bitcast.18, ...), custom_call_target="tpu_custom_call" | custom-call | tf_op jit(solution)/shard_map/spectral_analysis/pallas_call | solution.py:624
  36.7 2.1 %results.1 = (f32[4,256,128]{2,1,0:T(8,128)}, f32[4,256,128]{2,1,0:T(8,128)}, f32[20,384]{1,0:T(8,128)}) custom-call(f32[4,256,128]{2,1,0:T(8,128)} %get-tuple-element.9.refs_0_, f32[4,256,128]{2,1,0:T(8,128)} %get-tuple-element.10.refs_1_, f32[20,384]{1,0:T(8,128)} %get-tuple-element.11.refs_2_), custom_call_target="tpu_custom_call" | custom-call | tf_op jit(solution)/shard_map/results/pallas_call | solution.py:607

commit v5 on v4

--- a/solution.py
+++ b/solution.py
@@ -21,6 +21,8 @@
 HALF = 64
 TIMES = 4
 GROUP = 16
+PART = 32
+ROWS = 24
 PLANE = 8
 PLANES = 4
 MEMBERS = 128
@@ -159,7 +161,7 @@
     lax.fori_loop(1, BANDS, greet, 0)
 
 
-def legendre_sums(first, waits, spec, leg, degree_ref, columns, scaled, factor, sums):
+def legendre_sums(groups, first, waits, spec, leg, degree_ref, columns, scaled, factor, sums):
     spec_wait, leg_wait = waits
     lane = lax.broadcasted_iota(jnp.int32, (1, K), 1).astype(F32)
 
@@ -202,12 +204,12 @@
         lax.fori_loop(0, GROUP, one_slot, 0, unroll=GROUP)
         return carry
 
-    lax.fori_loop(0, SLOTS // GROUP, one_group, 0)
-
-
-def combine_rows(first, columns, rows_ref, sums, turned):
-    m = columns[pl.ds(first, SLOTS), :]
-    lanes = lax.broadcasted_iota(jnp.int32, (SLOTS, WIDTH), 1)
+    lax.fori_loop(groups[0], groups[1], one_group, 0)
+
+
+def combine_rows(start, first, columns, rows_ref, sums, turned):
+    m = columns[pl.ds(pl.multiple_of(first + start, PART), PART), :]
+    lanes = lax.broadcasted_iota(jnp.int32, (PART, WIDTH), 1)
     half_m = jnp.floor(m * 0.5)
     parity = 1.0 - 2.0 * (m - 2.0 * half_m)
     weight = jnp.where(m == 0.0, 1.0, 2.0)
@@ -228,9 +230,9 @@
     first_lane = (lanes == 0) | (lanes == HALF)
     last_lane = (lanes == HALF - 1) | (lanes == WIDTH - 1)
 
-    def one_time(t, carry):
+    def fields(t):
         def pieces(q):
-            c = sums[pl.ds(t * 4 + q, SLOTS, stride=16), :] * sign
+            c = sums[pl.ds(start * 16 + t * 4 + q, PART, stride=16), :] * sign
             before = jnp.where(first_lane, 0.0, pltpu.roll(c, 1, 1))
             after = jnp.where(last_lane, pltpu.roll(c, HALF, 1), pltpu.roll(c, WIDTH - 1, 1))
             return c * xx, (before + after - 2.0 * c) * yy, (before - after) * xy
@@ -242,27 +244,43 @@
         a = (pr_xx - ci_xy, pi_xx + cr_xy)
         b = (-ci_xy - pr_yy, cr_xy - pi_yy)
         normal = (2.0 * pi_xy + cr_xx - cr_yy, -2.0 * pr_xy + ci_xx - ci_yy)
-        for q, pair in enumerate((a, b, normal)):
-            block = jnp.concatenate(pair, axis=0).T
-            turned[q, pl.ds(t, WIDTH, stride=4), :] = block
-        return carry
-
-    lax.fori_loop(0, TIMES, one_time, 0, unroll=4)
+        return a, b, normal
+
+    for pair in range(TIMES // 2):
+        early, late = fields(2 * pair), fields(2 * pair + 1)
+        for q in range(3):
+            block = jnp.concatenate(early[q] + late[q], axis=0).T
+            turned[q, pl.ds(pair, WIDTH, stride=2), :] = block
 
 
 def build_onehot(wave_ref, onehot):
     lane = lax.broadcasted_iota(jnp.int32, (WIDTH, WIDTH), 1).astype(F32)
+    quarter = lax.broadcasted_iota(jnp.int32, (1, WIDTH), 1) // PART
 
     def one_block(j, carry):
-        column = column_of(wave_ref[pl.ds(j, 1), :].astype(F32))
-        rows = pl.ds(pl.multiple_of(j * WIDTH, WIDTH), WIDTH)
-        for tile in range(K // WIDTH):
-            onehot[rows, tile * WIDTH : (tile + 1) * WIDTH] = jnp.where(
-                column == lane + float(tile * WIDTH), 1.0, 0.0
-            ).astype(BF16)
+        a = wave_ref[pl.ds(2 * j, 1), :].astype(F32)
+        b = wave_ref[pl.ds(2 * j + 1, 1), :].astype(F32)
+        for part in range(2):
+            shift = PART * part
+            line = jnp.where(
+                quarter < 2,
+                jnp.where(quarter == 0, rolled(a, -shift), rolled(a, -PART - shift)),
+                jnp.where(quarter == 2, rolled(b, 64 - shift), rolled(b, PART - shift)),
+            )
+            column = column_of(line)
+            rows = pl.ds(pl.multiple_of(part * (K // 2) + j * WIDTH, WIDTH), WIDTH)
+            for tile in range(K // WIDTH):
+                onehot[rows, tile * WIDTH : (tile + 1) * WIDTH] = jnp.where(
+                    column == lane + float(tile * WIDTH), 1.0, 0.0
+                ).astype(BF16)
         return carry
 
-    lax.fori_loop(0, K // WIDTH, one_block, 0)
+    lax.fori_loop(0, K // (2 * WIDTH), one_block, 0)
+
+
+def rolled(value, shift):
+    shift = shift % WIDTH
+    return pltpu.roll(value, shift, 1) if shift else value
 
 
 def candidate_tables(owner_ref, block_ref, goal, named):
@@ -289,55 +307,56 @@
     named[...] = cells.T.astype(BF16)
 
 
-def join_plane(plane, coeffs, ordered_in):
-    pick = lax.broadcasted_iota(jnp.int32, (48, WIDTH), 1) < 64
-    for j in range(PLANE // 2):
-        a = coeffs[plane * PLANE + 2 * j].astype(F32)
-        b = coeffs[plane * PLANE + 2 * j + 1].astype(F32)
-        real = jnp.where(pick, a, pltpu.roll(b, 64, 1))
-        imag = jnp.where(pick, pltpu.roll(a, 64, 1), b)
-        ordered_in[0:48, j * WIDTH : (j + 1) * WIDTH] = real.astype(BF16)
-        ordered_in[48:96, j * WIDTH : (j + 1) * WIDTH] = imag.astype(BF16)
-
-
-def order_plane(plane, number, ordered_in, onehot, ordered, spread):
-    pick = lax.broadcasted_iota(jnp.int32, (8, WIDTH), 1) < 64
-    depth = PLANE * SLOTS
-    rows = pl.ds(pl.multiple_of(plane * depth, depth), depth)
+def join_quad(quad, coeffs, ordered_in, at):
+    quarter = lax.broadcasted_iota(jnp.int32, (ROWS, WIDTH), 1) // PART
+    sources = [coeffs[4 * quad + k].astype(F32) for k in range(4)]
+    rows = []
+    for c in range(2):
+        for x in range(2):
+            group = 2 * x + c
+            parts = [rolled(sources[k], (k - group) * PART) for k in range(4)]
+            rows.append(
+                jnp.where(
+                    quarter < 2,
+                    jnp.where(quarter == 0, parts[0], parts[1]),
+                    jnp.where(quarter == 2, parts[2], parts[3]),
+                )
+            )
+    ordered_in[:, at * WIDTH : (at + 1) * WIDTH] = jnp.concatenate(rows, axis=0).astype(BF16)
+
+
+def order_slots(start, depth, begin, last, ordered_in, onehot, ordered, spread):
+    pick = lax.broadcasted_iota(jnp.int32, (ROWS, WIDTH), 1) < 64
+    rows = pl.ds(start, depth)
     for j in range(8):
         at = slice(256 * j, 256 * (j + 1))
-        part = jnp.dot(ordered_in[...], onehot[rows, at], preferred_element_type=F32)
-        if number > 0:
+        part = jnp.dot(
+            ordered_in[:, :depth], onehot[rows, at], preferred_element_type=F32
+        )
+        if not begin:
             part = part + ordered[:, at]
-        if number < PLANES - 1:
+        if not last:
             ordered[:, at] = part
             continue
         for tile in range(2):
             h = 4 * j + 2 * tile
             for c in range(2):
-                for f in range(3):
-                    at = c * 48 + f * 16
-                    a = part[at : at + 8, tile * WIDTH : (tile + 1) * WIDTH]
-                    b = part[at + 8 : at + 16, tile * WIDTH : (tile + 1) * WIDTH]
-                    to = c * 24 + f * 8
-                    spread[h * 48 + to : h * 48 + to + 8, :] = jnp.where(
-                        pick, a, pltpu.roll(b, 64, 1)
-                    )
-                    spread[(h + 1) * 48 + to : (h + 1) * 48 + to + 8, :] = jnp.where(
-                        pick, pltpu.roll(a, 64, 1), b
-                    )
+                a = part[c * 48 : c * 48 + 24, tile * WIDTH : (tile + 1) * WIDTH]
+                b = part[c * 48 + 24 : c * 48 + 48, tile * WIDTH : (tile + 1) * WIDTH]
+                to = h * 48 + c * 24
+                spread[to : to + 24, :] = jnp.where(pick, a, pltpu.roll(b, 64, 1))
+                spread[to + 48 : to + 72, :] = jnp.where(pick, pltpu.roll(a, 64, 1), b)
 
 
 def synthesis(band, spread, tables, vort_out, okubo_out, table):
     first_ref, twiddle_ref, second_ref, fit_ref, fit_rows = tables
     southern = band >= BANDS // 2
-    for t in range(TIMES):
-        for rr in range(2):
-            row_low = jnp.where(southern, 3 - rr, rr)
-            row_high = jnp.where(southern, 1 - rr, 2 + rr)
+    for pair in range(TIMES // 2):
+        for r in range(4):
+            row = jnp.where(southern, 3 - r, r)
             parts = []
             for f in range(3):
-                i = f * 8 + rr * 4 + t
+                i = f * 8 + r * 2 + pair
                 c = jnp.concatenate(
                     [spread[pl.ds(i, 32, stride=48), :], spread[pl.ds(24 + i, 32, stride=48), :]],
                     axis=0,
@@ -361,24 +380,22 @@
             normal = grid[:, 2 * WIDTH :]
             vort = a - b
             okubo = normal * normal + 4.0 * (a * b)
-            vort_out[t, pl.ds(row_low, 64, stride=4), :] = vort[:64]
-            vort_out[t, pl.ds(row_high, 64, stride=4), :] = vort[64:]
-            okubo_out[t, pl.ds(row_low, 64, stride=4), :] = okubo[:64]
-            okubo_out[t, pl.ds(row_high, 64, stride=4), :] = okubo[64:]
+            for x in range(2):
+                half = slice(64 * x, 64 * x + 64)
+                vort_out[2 * pair + x, pl.ds(row, 64, stride=4), :] = vort[half]
+                okubo_out[2 * pair + x, pl.ds(row, 64, stride=4), :] = okubo[half]
             both = jnp.concatenate([vort, okubo], axis=1)
             high = both.astype(BF16)
             low = (both - high.astype(F32)).astype(BF16)
             from_high = jnp.dot(high, fit_ref[...], preferred_element_type=F32)
             from_low = jnp.dot(low, fit_ref[...], preferred_element_type=F32)
             fits = from_high + pltpu.roll(from_high, WIDTH - 32, 1) + from_low
-            fits = (
-                fits[:64] * fit_rows[pl.ds(row_low, 1), :]
-                + fits[64:] * fit_rows[pl.ds(row_high, 1), :]
-            )
-            if rr == 0:
-                table[t * 64 : (t + 1) * 64, :] = fits
+            fits = fits * fit_rows[pl.ds(row, 1), :]
+            window = slice(128 * pair, 128 * pair + 128)
+            if r == 0:
+                table[window, :] = fits
             else:
-                table[t * 64 : (t + 1) * 64, :] += fits
+                table[window, :] += fits
 
 
 def pick_candidates(goal, named, table):
@@ -476,42 +493,61 @@
     columns[...] = column_of(wave_ref[pl.ds(me // 2, 1), :].astype(F32))
     first = pl.multiple_of(lax.rem(me, 2) * SLOTS, SLOTS)
     waits = (lambda g: spec_copy(g).wait(), lambda g: leg_copy(g).wait())
-    legendre_sums(first, waits, spec, leg, degree_ref, columns, scaled, factor, sums)
-    combine_rows(first, columns, rows_ref, sums, turned)
-
-    for p in range(BANDS):
-        for q in range(3):
-            send[p, 16 * q : 16 * q + 16, :] = turned[q, p * 16 : p * 16 + 16, :].astype(BF16)
-
-    pl.semaphore_wait(barrier, BANDS - 1 + LEVS - 1)
-
     my_plane = me // PLANE
     my_place = lax.rem(me, PLANE)
+    shifts = (0, 1, 3, 2)
 
     def place(d):
         return jnp.where(d < BANDS // 2, d, BANDS + BANDS // 2 - 1 - d)
 
-    shifts = (0, 1, 3, 2)
-    for number, shift in enumerate(shifts):
-        plane = lax.rem(my_plane + shift, PLANES)
-        for k in range(0 if shift else 1, PLANE):
-            d = plane * PLANE + lax.rem(my_place + k, PLANE)
-            pltpu.make_async_remote_copy(
-                src_ref=send.at[place(d)],
-                dst_ref=recv.at[me],
-                send_sem=send_sem,
-                recv_sem=recv_sem.at[number],
-                device_id={"lev": lev, "band": d},
-                device_id_type=MESH,
-            ).start()
-    recv[me] = send[place(me)]
+    def one_half(half, carry):
+        legendre_sums(
+            (2 * half, 2 * half + 2),
+            first,
+            waits,
+            spec,
+            leg,
+            degree_ref,
+            columns,
+            scaled,
+            factor,
+            sums,
+        )
+        combine_rows(
+            pl.multiple_of(half * PART, PART), first, columns, rows_ref, sums, turned
+        )
+        for p in range(BANDS):
+            send[half, p] = jnp.concatenate(
+                [turned[q, p * 8 : p * 8 + 8, :] for q in range(3)], axis=0
+            ).astype(BF16)
+
+        @pl.when(half == 0)
+        def _():
+            pl.semaphore_wait(barrier, BANDS - 1 + LEVS - 1)
+
+        for number, shift in enumerate(shifts):
+            plane = lax.rem(my_plane + shift, PLANES)
+            for k in range(0 if shift else 1, PLANE):
+                d = plane * PLANE + lax.rem(my_place + k, PLANE)
+                pltpu.make_async_remote_copy(
+                    src_ref=send.at[half, place(d)],
+                    dst_ref=recv.at[half, me],
+                    send_sem=send_sem.at[half],
+                    recv_sem=recv_sem.at[half * (1 + number)],
+                    device_id={"lev": lev, "band": d},
+                    device_id_type=MESH,
+                ).start()
+        recv[half, me] = send[half, place(me)]
+        return carry
+
+    lax.fori_loop(0, 2, one_half, 0)
     greet_peers(level_sem, lev, me)
 
-    def bulk(count, number):
+    def bulk(half, count, number):
         return pltpu.make_async_remote_copy(
-            src_ref=send.at[pl.ds(0, count)],
-            dst_ref=recv.at[pl.ds(0, count)],
-            send_sem=send_sem,
+            src_ref=send.at[half, pl.ds(0, count)],
+            dst_ref=recv.at[half, pl.ds(0, count)],
+            send_sem=send_sem.at[half],
             recv_sem=recv_sem.at[number],
             device_id={"lev": lev, "band": me},
             device_id_type=MESH,
@@ -520,11 +556,20 @@
     build_onehot(wave_ref, onehot)
     candidate_tables(owner_ref, block_ref, goal, named)
 
+    bulk(0, BANDS - 1, 0).wait_recv()
+    for quad in range(PLANE):
+        join_quad(quad, recv.at[0], ordered_in, quad)
+    order_slots(0, K // 2, True, False, ordered_in, onehot, ordered, spread)
+    depth = PLANE * PART
     for number, shift in enumerate(shifts):
         plane = lax.rem(my_plane + PLANES - shift, PLANES)
-        bulk(PLANE if shift else PLANE - 1, number).wait_recv()
-        join_plane(plane, recv, ordered_in)
-        order_plane(plane, number, ordered_in, onehot, ordered, spread)
+        bulk(1, PLANE if shift else PLANE - 1, 1 + number).wait_recv()
+        for k in range(2):
+            join_quad(2 * plane + k, recv.at[1], ordered_in, k)
+        start = pl.multiple_of(K // 2 + plane * depth, depth)
+        order_slots(
+            start, depth, False, number == PLANES - 1, ordered_in, onehot, ordered, spread
+        )
 
     tables = (first_ref, twiddle_ref, second_ref, fit_ref, fit_rows)
     synthesis(me, spread, tables, vort, okubo, table)
@@ -572,7 +617,8 @@
             lines[pl.ds(PACK * r + g, BANDS, stride=CAP), :] = value
     fits_out[...] = lines[...].T[:20, :]
 
-    bulk(BANDS - 1, 0).wait_send()
+    bulk(0, BANDS - 1, 0).wait_send()
+    bulk(1, BANDS - 1, 0).wait_send()
     everything.wait_send()
     for copy in grid_copies:
         copy.wait()
@@ -633,13 +679,13 @@
             pltpu.VMEM((GROUP, K), F32),
             pltpu.VMEM((WIDTH, WIDTH), F32),
             pltpu.VMEM((SLOTS * 16, WIDTH), F32),
-            pltpu.VMEM((3, 4 * WIDTH, WIDTH), F32),
-            pltpu.VMEM((BANDS, 48, WIDTH), BF16),
-            pltpu.VMEM((BANDS, 48, WIDTH), BF16),
+            pltpu.VMEM((3, 2 * WIDTH, WIDTH), F32),
+            pltpu.VMEM((2, BANDS, ROWS, WIDTH), BF16),
+            pltpu.VMEM((2, BANDS, ROWS, WIDTH), BF16),
             pltpu.VMEM((K, K), BF16),
             pltpu.VMEM((PACK * 2 * BANDS, CANDS), BF16),
             pltpu.VMEM((CANDS, 256), BF16),
-            pltpu.VMEM((96, PLANE * SLOTS), BF16),
+            pltpu.VMEM((96, K // 2), BF16),
             pltpu.VMEM((96, K), F32),
             pltpu.VMEM((32 * 48, WIDTH), F32),
             pltpu.VMEM((TIMES, 256, WIDTH), F32),
@@ -650,8 +696,8 @@
             pltpu.VMEM((BANDS * CAP, WIDTH), F32),
             pltpu.SemaphoreType.DMA((SLOTS // GROUP,)),
             pltpu.SemaphoreType.DMA((SLOTS // GROUP,)),
-            pltpu.SemaphoreType.DMA,
-            pltpu.SemaphoreType.DMA((PLANES,)),
+            pltpu.SemaphoreType.DMA((2,)),
+            pltpu.SemaphoreType.DMA((1 + PLANES,)),
             pltpu.SemaphoreType.DMA,
             pltpu.SemaphoreType.DMA,
             pltpu.SemaphoreType.REGULAR,

time: 39 us -> 37.7 us (0.967)
  Pallas kernels: 38.2 us -> 36.9 us
    pallas_call x1, Pallas kernels: 36.1 us -> 34.8 us  [whole(): pl.pallas_call(whole_kernel, out_shape=(grid, grid, jax.ShapeDtypeStruct(...]
where the time goes in v5:
time: 37.7 us; the launch traced here: 37.5 us
  Pallas kernels  36.9 us (98%)
  between operations  0.64 us (2%)
    pallas_call x1, Pallas kernels, whole(): pl.pallas_call(whole_kernel, out_shape=(grid, grid, jax.ShapeDtypeStruct(...  34.8 us
    pallas_call x1, Pallas kernels, copied(): pl.pallas_call(copy_kernel, out_shape=tuple((jax.ShapeDtypeStruct(r.shape...  2.11 us

profile of v5, /device:TPU:1, one launch (start us, length us, event | category | flops | bytes accessed | tf_op | source)
XLA Modules:
  0.0 37.5 jit_solution(16351138969154192454)
XLA Ops:
  0.6 34.8 %spectral_analysis.1 = (f32[4,256,128]{2,1,0:T(8,128)}, f32[4,256,128]{2,1,0:T(8,128)}, f32[20,384]{1,0:T(8,128)}) custom-call(bf16[16,64,2048]{2,1,0:T(8,128)(2,1)} %bitcast.15, bf16[64,64,2048]{2,1,0:T(8,128)(2,1)} %leg_hbm.1, s32[16,128]{1,0:T(8,128)} %bitcast.16, s32[1,192]{1,0:T(1,128)} %bitcast.17, s32[1,192]{1,0:T(1,128)} %bitcast.18, ...), custom_call_target="tpu_custom_call" | custom-call | tf_op jit(solution)/shard_map/spectral_analysis/pallas_call | solution.py:670
  35.4 2.1 %results.1 = (f32[4,256,128]{2,1,0:T(8,128)}, f32[4,256,128]{2,1,0:T(8,128)}, f32[20,384]{1,0:T(8,128)}) custom-call(f32[4,256,128]{2,1,0:T(8,128)} %get-tuple-element.9.refs_0_, f32[4,256,128]{2,1,0:T(8,128)} %get-tuple-element.10.refs_1_, f32[20,384]{1,0:T(8,128)} %get-tuple-element.11.refs_2_), custom_call_target="tpu_custom_call" | custom-call | tf_op jit(solution)/shard_map/results/pallas_call | solution.py:653

commit v6 on v5

--- a/solution.py
+++ b/solution.py
@@ -348,54 +348,57 @@
                 spread[to + 48 : to + 72, :] = jnp.where(pick, pltpu.roll(a, 64, 1), b)
 
 
-def synthesis(band, spread, tables, vort_out, okubo_out, table):
+def synthesis(band, spread, tables, vort_out, okubo_out, table, stage, cells):
     first_ref, twiddle_ref, second_ref, fit_ref, fit_rows = tables
     southern = band >= BANDS // 2
+    steps = [(pair, r) for pair in range(TIMES // 2) for r in range(4)]
+    tc, ts = twiddle_ref[0], twiddle_ref[1]
+    for n, (pair, r) in enumerate(steps):
+        for f in range(3):
+            i = f * 8 + r * 2 + pair
+            c = jnp.concatenate(
+                [spread[pl.ds(i, 32, stride=48), :], spread[pl.ds(24 + i, 32, stride=48), :]],
+                axis=0,
+            ).T.astype(BF16)
+            z = jnp.dot(
+                jnp.concatenate([c, c], axis=1), first_ref[...], preferred_element_type=F32
+            )
+            zr, zi = z[:, :WIDTH], z[:, WIDTH:]
+            z = jnp.concatenate([zr * tc - zi * ts, zr * ts + zi * tc], axis=0)
+            high = z.astype(BF16)
+            low = (z - high.astype(F32)).astype(BF16)
+            at = slice(f * WIDTH, (f + 1) * WIDTH)
+            stage[n, 0:256, at] = high
+            stage[n, 256:512, at] = low
+    for n, (pair, r) in enumerate(steps):
+        row = jnp.where(southern, 3 - r, r)
+        grid = jnp.dot(
+            second_ref[...],
+            jnp.concatenate([stage[n, 0:256, :], stage[n]], axis=0),
+            preferred_element_type=F32,
+        )
+        a = grid[:, :WIDTH]
+        b = grid[:, WIDTH : 2 * WIDTH]
+        normal = grid[:, 2 * WIDTH :]
+        vort = a - b
+        okubo = normal * normal + 4.0 * (a * b)
+        for x in range(2):
+            half = slice(64 * x, 64 * x + 64)
+            vort_out[2 * pair + x, pl.ds(row, 64, stride=4), :] = vort[half]
+            okubo_out[2 * pair + x, pl.ds(row, 64, stride=4), :] = okubo[half]
+        both = jnp.concatenate([vort, okubo], axis=1)
+        high = both.astype(BF16)
+        cells[n, 0:128, :] = high
+        cells[n, 128:256, :] = (both - high.astype(F32)).astype(BF16)
     for pair in range(TIMES // 2):
+        total = jnp.zeros((WIDTH, WIDTH), F32)
         for r in range(4):
             row = jnp.where(southern, 3 - r, r)
-            parts = []
-            for f in range(3):
-                i = f * 8 + r * 2 + pair
-                c = jnp.concatenate(
-                    [spread[pl.ds(i, 32, stride=48), :], spread[pl.ds(24 + i, 32, stride=48), :]],
-                    axis=0,
-                ).T.astype(BF16)
-                z = jnp.dot(
-                    jnp.concatenate([c, c], axis=1), first_ref[...], preferred_element_type=F32
-                )
-                zr, zi = z[:, :WIDTH], z[:, WIDTH:]
-                tc, ts = twiddle_ref[0], twiddle_ref[1]
-                parts.append(jnp.concatenate([zr * tc - zi * ts, zr * ts + zi * tc], axis=0))
-            z = jnp.concatenate(parts, axis=1)
-            high = z.astype(BF16)
-            low = (z - high.astype(F32)).astype(BF16)
-            grid = jnp.dot(
-                second_ref[...],
-                jnp.concatenate([high, high, low], axis=0),
-                preferred_element_type=F32,
-            )
-            a = grid[:, :WIDTH]
-            b = grid[:, WIDTH : 2 * WIDTH]
-            normal = grid[:, 2 * WIDTH :]
-            vort = a - b
-            okubo = normal * normal + 4.0 * (a * b)
-            for x in range(2):
-                half = slice(64 * x, 64 * x + 64)
-                vort_out[2 * pair + x, pl.ds(row, 64, stride=4), :] = vort[half]
-                okubo_out[2 * pair + x, pl.ds(row, 64, stride=4), :] = okubo[half]
-            both = jnp.concatenate([vort, okubo], axis=1)
-            high = both.astype(BF16)
-            low = (both - high.astype(F32)).astype(BF16)
-            from_high = jnp.dot(high, fit_ref[...], preferred_element_type=F32)
-            from_low = jnp.dot(low, fit_ref[...], preferred_element_type=F32)
-            fits = from_high + pltpu.roll(from_high, WIDTH - 32, 1) + from_low
-            fits = fits * fit_rows[pl.ds(row, 1), :]
-            window = slice(128 * pair, 128 * pair + 128)
-            if r == 0:
-                table[window, :] = fits
-            else:
-                table[window, :] += fits
+            both = jnp.dot(cells[4 * pair + r], fit_ref[...], preferred_element_type=F32)
+            high, low = both[:WIDTH], both[WIDTH:]
+            fits = high + pltpu.roll(high, WIDTH - 32, 1) + low
+            total += fits * fit_rows[pl.ds(row, 1), :]
+        table[128 * pair : 128 * pair + 128, :] = total
 
 
 def pick_candidates(goal, named, table):
@@ -425,6 +428,19 @@
 def whole_kernel(
     spec_hbm,
     leg_hbm,
+    wave_hbm,
+    owner_hbm,
+    block_hbm,
+    degree_hbm,
+    rows_hbm,
+    first_hbm,
+    twiddle_hbm,
+    second_hbm,
+    fit_hbm,
+    fit_rows_hbm,
+    vort_out,
+    okubo_out,
+    fits_out,
     wave_ref,
     owner_ref,
     block_ref,
@@ -435,9 +451,6 @@
     second_ref,
     fit_ref,
     fit_rows,
-    vort_out,
-    okubo_out,
-    fits_out,
     spec,
     leg,
     scaled,
@@ -456,6 +469,8 @@
     vort,
     okubo,
     table,
+    stage,
+    cells,
     outgoing,
     arrived,
     lines,
@@ -467,6 +482,7 @@
     recv_fit,
     level_sem,
     out_sem,
+    table_sem,
 ):
     lev = lax.axis_index("lev")
     me = lax.axis_index("band")
@@ -482,14 +498,37 @@
         window = pl.ds(pl.multiple_of(g * GROUP, GROUP), GROUP)
         return pltpu.make_async_copy(leg_hbm.at[window], leg.at[window], leg_sem.at[g])
 
+    table_copies = [
+        pltpu.make_async_copy(source, target, table_sem.at[n])
+        for n, (source, target) in enumerate(
+            (
+                (wave_hbm, wave_ref),
+                (degree_hbm, degree_ref),
+                (rows_hbm, rows_ref),
+                (owner_hbm, owner_ref),
+                (block_hbm, block_ref),
+                (first_hbm, first_ref),
+                (twiddle_hbm, twiddle_ref),
+                (second_hbm, second_ref),
+                (fit_hbm, fit_ref),
+                (fit_rows_hbm, fit_rows),
+            )
+        )
+    ]
+    for copy in table_copies[:3]:
+        copy.start()
     for g in range(SLOTS // GROUP):
         spec_copy(g).start()
         leg_copy(g).start()
+    for copy in table_copies[3:]:
+        copy.start()
 
     barrier = pltpu.get_barrier_semaphore()
     greet_peers(barrier, lev, me)
     greet_band(barrier, lev, me)
 
+    for copy in table_copies[:3]:
+        copy.wait()
     columns[...] = column_of(wave_ref[pl.ds(me // 2, 1), :].astype(F32))
     first = pl.multiple_of(lax.rem(me, 2) * SLOTS, SLOTS)
     waits = (lambda g: spec_copy(g).wait(), lambda g: leg_copy(g).wait())
@@ -554,6 +593,8 @@
         )
 
     build_onehot(wave_ref, onehot)
+    for copy in table_copies[3:]:
+        copy.wait()
     candidate_tables(owner_ref, block_ref, goal, named)
 
     bulk(0, BANDS - 1, 0).wait_recv()
@@ -572,7 +613,7 @@
         )
 
     tables = (first_ref, twiddle_ref, second_ref, fit_ref, fit_rows)
-    synthesis(me, spread, tables, vort, okubo, table)
+    synthesis(me, spread, tables, vort, okubo, table, stage, cells)
     grid_copies = [
         pltpu.make_async_copy(vort, vort_out, out_sem.at[0]),
         pltpu.make_async_copy(okubo, okubo_out, out_sem.at[1]),
@@ -670,9 +711,19 @@
     return pl.pallas_call(
         whole_kernel,
         out_shape=(grid, grid, jax.ShapeDtypeStruct((20, BANDS * CAP), F32)),
-        in_specs=[hbm, hbm] + [vmem] * 10,
+        in_specs=[hbm] * 12,
         out_specs=(hbm, hbm, vmem),
         scratch_shapes=[
+            pltpu.VMEM((K // WIDTH, WIDTH), jnp.int32),
+            pltpu.VMEM((1, CANDS), jnp.int32),
+            pltpu.VMEM((1, CANDS), jnp.int32),
+            pltpu.VMEM((8, K), F32),
+            pltpu.VMEM((8, WIDTH), F32),
+            pltpu.VMEM((WIDTH, 2 * WIDTH), BF16),
+            pltpu.VMEM((2, WIDTH, WIDTH), F32),
+            pltpu.VMEM((WIDTH, 6 * WIDTH), BF16),
+            pltpu.VMEM((2 * WIDTH, WIDTH), BF16),
+            pltpu.VMEM((8, WIDTH), F32),
             pltpu.VMEM((16, SLOTS, K), BF16),
             pltpu.VMEM((SLOTS, HALF, K), BF16),
             pltpu.VMEM((K // WIDTH, 16 * GROUP, WIDTH), F32),
@@ -691,6 +742,8 @@
             pltpu.VMEM((TIMES, 256, WIDTH), F32),
             pltpu.VMEM((TIMES, 256, WIDTH), F32),
             pltpu.VMEM((256, WIDTH), F32),
+            pltpu.VMEM((8, 512, 3 * WIDTH), BF16),
+            pltpu.VMEM((8, 256, 256), BF16),
             pltpu.VMEM((BANDS, 2, WIDTH), F32),
             pltpu.VMEM((MEMBERS, 2, WIDTH), F32),
             pltpu.VMEM((BANDS * CAP, WIDTH), F32),
@@ -702,6 +755,7 @@
             pltpu.SemaphoreType.DMA,
             pltpu.SemaphoreType.REGULAR,
             pltpu.SemaphoreType.DMA((2,)),
+            pltpu.SemaphoreType.DMA((10,)),
         ],
         compiler_params=pltpu.CompilerParams(
             collective_id=0, has_side_effects=True, vmem_limit_bytes=56 * 1024 * 1024

time: 37.7 us -> 35.6 us (0.944)
  Pallas kernels: 36.9 us -> 34.8 us
    pallas_call x1, Pallas kernels: 34.8 us -> 32.7 us  [whole(): pl.pallas_call(whole_kernel, out_shape=(grid, grid, jax.ShapeDtypeStruct(...]
where the time goes in v6:
time: 35.6 us; the launch traced here: 35.5 us
  Pallas kernels  34.8 us (98%)
  between operations  0.64 us (2%)
    pallas_call x1, Pallas kernels, whole(): pl.pallas_call(whole_kernel, out_shape=(grid, grid, jax.ShapeDtypeStruct(...  32.7 us
    pallas_call x1, Pallas kernels, copied(): pl.pallas_call(copy_kernel, out_shape=tuple((jax.ShapeDtypeStruct(r.shape...  2.11 us

profile of v6, /device:TPU:1, one launch (start us, length us, event | category | flops | bytes accessed | tf_op | source)
XLA Modules:
  0.0 35.5 jit_solution(13102070896546752290)
XLA Ops:
  0.6 32.7 %spectral_analysis.1 = (f32[4,256,128]{2,1,0:T(8,128)}, f32[4,256,128]{2,1,0:T(8,128)}, f32[20,384]{1,0:T(8,128)}) custom-call(bf16[16,64,2048]{2,1,0:T(8,128)(2,1)} %bitcast.15, bf16[64,64,2048]{2,1,0:T(8,128)(2,1)} %leg_hbm.1, s32[16,128]{1,0:T(8,128)} %bitcast.16, s32[1,192]{1,0:T(1,128)} %bitcast.17, s32[1,192]{1,0:T(1,128)} %bitcast.18, ...), custom_call_target="tpu_custom_call" | custom-call | tf_op jit(solution)/shard_map/spectral_analysis/pallas_call | solution.py:711
  33.4 2.1 %results.1 = (f32[4,256,128]{2,1,0:T(8,128)}, f32[4,256,128]{2,1,0:T(8,128)}, f32[20,384]{1,0:T(8,128)}) custom-call(f32[4,256,128]{2,1,0:T(8,128)} %get-tuple-element.9.refs_0_, f32[4,256,128]{2,1,0:T(8,128)} %get-tuple-element.10.refs_1_, f32[20,384]{1,0:T(8,128)} %get-tuple-element.11.refs_2_), custom_call_target="tpu_custom_call" | custom-call | tf_op jit(solution)/shard_map/results/pallas_call | solution.py:694

commit v7 on v6

--- a/solution.py
+++ b/solution.py
@@ -207,9 +207,9 @@
     lax.fori_loop(groups[0], groups[1], one_group, 0)
 
 
-def combine_rows(start, first, columns, rows_ref, sums, turned):
-    m = columns[pl.ds(pl.multiple_of(first + start, PART), PART), :]
-    lanes = lax.broadcasted_iota(jnp.int32, (PART, WIDTH), 1)
+def row_weights(first, columns, rows_ref, weights):
+    m = columns[pl.ds(first, SLOTS), :]
+    lanes = lax.broadcasted_iota(jnp.int32, (SLOTS, WIDTH), 1)
     half_m = jnp.floor(m * 0.5)
     parity = 1.0 - 2.0 * (m - 2.0 * half_m)
     weight = jnp.where(m == 0.0, 1.0, 2.0)
@@ -226,6 +226,13 @@
     )
     xx = -4.0 * sin * sin * rows_ref[0:1, :]
     xy = 2.0 * (2.0 * sin * cos) * rows_ref[1:2, :]
+    weights[0], weights[1], weights[2] = sign, xx, xy
+
+
+def combine_rows(start, weights, rows_ref, sums, turned):
+    window = pl.ds(start, PART)
+    sign, xx, xy = weights[0, window, :], weights[1, window, :], weights[2, window, :]
+    lanes = lax.broadcasted_iota(jnp.int32, (PART, WIDTH), 1)
     yy = rows_ref[2:3, :]
     first_lane = (lanes == 0) | (lanes == HALF)
     last_lane = (lanes == HALF - 1) | (lanes == WIDTH - 1)
@@ -410,19 +417,12 @@
         jnp.concatenate([high, low], axis=1).astype(BF16),
         preferred_element_type=F32,
     )
-    total = jnp.zeros((2 * BANDS, 2 * WIDTH), F32)
-    for g in range(PACK):
-        high = chosen[:, :WIDTH]
-        low = chosen[:, WIDTH:]
-        if g:
-            high = pltpu.roll(high, VALUES * g, 1)
-            low = pltpu.roll(low, VALUES * g, 1)
-        total += jnp.dot(
-            goal[g * 2 * BANDS : (g + 1) * 2 * BANDS, :],
-            jnp.concatenate([high, low], axis=1).astype(BF16),
-            preferred_element_type=F32,
-        )
-    return total[:, :WIDTH] + total[:, WIDTH:]
+    parts = jnp.dot(goal[...], chosen.astype(BF16), preferred_element_type=F32)
+    parts = parts[:, :WIDTH] + parts[:, WIDTH:]
+    total = parts[: 2 * BANDS]
+    for g in range(1, PACK):
+        total += pltpu.roll(parts[2 * BANDS * g : 2 * BANDS * (g + 1)], VALUES * g, 1)
+    return total
 
 
 def whole_kernel(
@@ -456,6 +456,7 @@
     scaled,
     factor,
     columns,
+    weights,
     sums,
     turned,
     send,
@@ -473,6 +474,7 @@
     cells,
     outgoing,
     arrived,
+    joined,
     lines,
     spec_sem,
     leg_sem,
@@ -531,6 +533,7 @@
         copy.wait()
     columns[...] = column_of(wave_ref[pl.ds(me // 2, 1), :].astype(F32))
     first = pl.multiple_of(lax.rem(me, 2) * SLOTS, SLOTS)
+    row_weights(first, columns, rows_ref, weights)
     waits = (lambda g: spec_copy(g).wait(), lambda g: leg_copy(g).wait())
     my_plane = me // PLANE
     my_place = lax.rem(me, PLANE)
@@ -553,7 +556,7 @@
             sums,
         )
         combine_rows(
-            pl.multiple_of(half * PART, PART), first, columns, rows_ref, sums, turned
+            pl.multiple_of(half * PART, PART), weights, rows_ref, sums, turned
         )
         for p in range(BANDS):
             send[half, p] = jnp.concatenate(
@@ -637,7 +640,7 @@
         ).start()
         return carry
 
-    lax.fori_loop(1, MEMBERS, post_fit, 0, unroll=4)
+    lax.fori_loop(1, MEMBERS, post_fit, 0, unroll=16)
     arrived[rank] = outgoing[me]
     everything = pltpu.make_async_remote_copy(
         src_ref=arrived.at[pl.ds(0, MEMBERS - 1)],
@@ -649,10 +652,9 @@
     )
     everything.wait_recv()
 
+    joined[...] = (arrived[0:32] + arrived[32:64]) + (arrived[64:96] + arrived[96:128])
     for r in range(CAP // PACK):
-        line = (arrived[0:32, r, :] + arrived[32:64, r, :]) + (
-            arrived[64:96, r, :] + arrived[96:128, r, :]
-        )
+        line = joined[:, r, :]
         for g in range(PACK):
             value = pltpu.roll(line, WIDTH - VALUES * g, 1) if g else line
             lines[pl.ds(PACK * r + g, BANDS, stride=CAP), :] = value
@@ -729,6 +731,7 @@
             pltpu.VMEM((K // WIDTH, 16 * GROUP, WIDTH), F32),
             pltpu.VMEM((GROUP, K), F32),
             pltpu.VMEM((WIDTH, WIDTH), F32),
+            pltpu.VMEM((3, SLOTS, WIDTH), F32),
             pltpu.VMEM((SLOTS * 16, WIDTH), F32),
             pltpu.VMEM((3, 2 * WIDTH, WIDTH), F32),
             pltpu.VMEM((2, BANDS, ROWS, WIDTH), BF16),
@@ -746,6 +749,7 @@
             pltpu.VMEM((8, 256, 256), BF16),
             pltpu.VMEM((BANDS, 2, WIDTH), F32),
             pltpu.VMEM((MEMBERS, 2, WIDTH), F32),
+            pltpu.VMEM((BANDS, 2, WIDTH), F32),
             pltpu.VMEM((BANDS * CAP, WIDTH), F32),
             pltpu.SemaphoreType.DMA((SLOTS // GROUP,)),
             pltpu.SemaphoreType.DMA((SLOTS // GROUP,)),

time: 35.6 us -> 35.6 us (level)
  no operation moved by 1% of the time
where the time goes in v7:
time: 35.6 us; the launch traced here: 35.5 us
  Pallas kernels  34.8 us (98%)
  between operations  0.64 us (2%)
    pallas_call x1, Pallas kernels, whole(): pl.pallas_call(whole_kernel, out_shape=(grid, grid, jax.ShapeDtypeStruct(...  32.7 us
    pallas_call x1, Pallas kernels, copied(): pl.pallas_call(copy_kernel, out_shape=tuple((jax.ShapeDtypeStruct(r.shape...  2.11 us

profile of v7, /device:TPU:1, one launch (start us, length us, event | category | flops | bytes accessed | tf_op | source)
XLA Modules:
  0.0 35.5 jit_solution(2097897935878506353)
XLA Ops:
  0.6 32.7 %spectral_analysis.1 = (f32[4,256,128]{2,1,0:T(8,128)}, f32[4,256,128]{2,1,0:T(8,128)}, f32[20,384]{1,0:T(8,128)}) custom-call(bf16[16,64,2048]{2,1,0:T(8,128)(2,1)} %bitcast.15, bf16[64,64,2048]{2,1,0:T(8,128)(2,1)} %leg_hbm.1, s32[16,128]{1,0:T(8,128)} %bitcast.16, s32[1,192]{1,0:T(1,128)} %bitcast.17, s32[1,192]{1,0:T(1,128)} %bitcast.18, ...), custom_call_target="tpu_custom_call" | custom-call | tf_op jit(solution)/shard_map/spectral_analysis/pallas_call | solution.py:713
  33.3 2.1 %results.1 = (f32[4,256,128]{2,1,0:T(8,128)}, f32[4,256,128]{2,1,0:T(8,128)}, f32[20,384]{1,0:T(8,128)}) custom-call(f32[4,256,128]{2,1,0:T(8,128)} %get-tuple-element.9.refs_0_, f32[4,256,128]{2,1,0:T(8,128)} %get-tuple-element.10.refs_1_, f32[20,384]{1,0:T(8,128)} %get-tuple-element.11.refs_2_), custom_call_target="tpu_custom_call" | custom-call | tf_op jit(solution)/shard_map/results/pallas_call | solution.py:696
